TPU v7x, 256 devices: a whole 4x4x8 slice. The times are simulated.
256 devices in a mesh: grp: 8 (over y, core), seg: 32 (over z, x).
Axes of the slice: x: 4, y: 4, z: 8, core: 2. Of those that a mesh axis runs over, the one named last changes fastest.
Arguments:
- queries: bfloat16 [8, 128, 8192], P('grp', 'seg'), may hold values from -96 to 96
- keys: bfloat16 [8, 4096, 1024], P('grp', 'seg'), may hold values from -6 to 6
- values: bfloat16 [8, 4096, 1024], P('grp', 'seg'), may hold values from -6 to 6
- node_ids: int32 [8, 4096], P('grp'), may hold values from 0 to 127, never falling along the last dimension, each value on 1 to 96 neighbouring positions
- parents: int32 [8, 128], P('grp'), may hold values from 0 to 126, as said below
- score_pos: int32 [8, 128], P('grp'), may hold values from 0 to 4095, as said below
- out_weight: bfloat16 [8192, 5120], P('seg'), may hold values from -0.0625 to 0.0625
- resid: bfloat16 [8, 128, 5120], P('grp', 'seg'), may hold values from -6 to 6
- norm_gain: bfloat16 [5120], replicated, may hold values from 0.5 to 1.5
- vocab_weight: bfloat16 [5120, 98304], P(None, ('grp', 'seg')), may hold values from -8 to 8
- targets: int32 [8, 128], P('grp', 'seg'), may hold values from 0 to 98303
- old_logp: float32 [8, 128], P('grp', 'seg'), may hold values from -18.5 to -13.5
- leaf_node: int32 [8, 64], P('grp'), may hold values from 0 to 127
- advantages: float32 [8, 64], P('grp', 'seg'), may hold values from -4 to 4
Outputs:
- token_logratio: float32 [8, 128], P('grp', 'seg')
- leaf_logratio: float32 [8, 64], P('grp', 'seg')
- loss: float32 [], replicated
Inputs may be any that keep to these rules, and one draw needn't show every extreme that they name: `parents`: node n's parent is n when n is a multiple of 8, the root of a tree of 8 consecutive nodes; otherwise an earlier node of the same tree, and the last node of each tree has the node before it as parent. `score_pos`: scored row r lies in packed positions (r // 4) * 128 to (r // 4 + 1) * 128 - 1; a group's first scored row is at position 0 and its last at 4095.
All inputs are finite; a program needn't handle non-finite values.
Results may differ from a plain program's by a relative error of at most 0.0095.
Values may be sent and summed in bfloat16 or wider, within the bound.
A program may use at most 128 MiB of HBM per device.

v0:
```python
import jax
import jax.numpy as jnp
from jax import lax
from jax.experimental import pallas as pl
from jax.experimental.pallas import tpu as pltpu
from jax.sharding import PartitionSpec as P

F32 = jnp.float32
BF16 = jnp.bfloat16
EPS_LOW = 0.0003
EPS_HIGH = 0.0004
NEGATIVE = -1e30
HEAD = 128
KV_HEADS = 8
X, Y, Z = 4, 4, 8
SEG = X * Z
GRP = 2 * Y
TOK = 128
ROWS = 128
NODES = 128
LEAVES = 64
SCORE = 4
WINDOW = 7
SLOTS = 8
D = 5120
DX = D // X
VOC = 384
CHUNKS = 4
CROWS = ROWS // CHUNKS
PARTS = ((0, 512, "xyz"), (512, 384, "yzx"), (896, 384, "zxy"))
MIB = 1024 * 1024


def iota(shape, dim):
    return lax.broadcasted_iota(jnp.int32, shape, dim)


def hot(mask):
    return mask.astype(F32).astype(BF16)


def mm(a, b):
    return jnp.dot(a, b, preferred_element_type=F32)


def mm_nt(a, b):
    return lax.dot_general(a, b, (((1,), (1,)), ((), ())), preferred_element_type=F32)


def closure_transposed(parent_row):
    sub = iota((NODES, NODES), 0)
    lane = iota((NODES, NODES), 1)
    step = jnp.where((sub == parent_row) | (sub == lane), 1.0, 0.0)
    for squaring in range(3):
        half = step.astype(BF16)
        step = jnp.minimum(mm(half, half), 1.0)
    return step.astype(BF16)


def scored_nodes(node_table, position_row):
    table = jnp.concatenate([node_table.astype(F32), jnp.zeros((TOK - SEG, TOK), F32)], axis=0)
    across = table.T.astype(BF16)
    sub = iota((TOK, ROWS), 0)
    lane = iota((TOK, ROWS), 1)
    spread = mm(across, hot(sub == lane // SCORE))
    match = sub == position_row - TOK * (lane // SCORE)
    return jnp.sum(jnp.where(match, spread, 0.0), axis=0, keepdims=True)


def attend_body(
    q_ref, k_ref, v_ref, node_ref, par_ref, pos_ref, ow_hbm, resid_ref, gain_ref,
    normed_ref,
    ow, qbuf, raised, parts, osend, obuf, aug, xsend, xown, xrecv, zsend, zown, zrecv, sqs, sqr,
    ow_sem, q_ss, q_rs, p_ss, p_rs, o_ss, o_rs, x_ss, x_rs, z_ss, z_rs, s_ss, s_rs,
):
    me = lax.axis_index("seg")
    z = me // X
    x = lax.rem(me, X)

    def at_x(delta):
        return {"seg": z * X + lax.rem(x + delta, X)}

    def at_z(delta):
        return {"seg": lax.rem(z + delta, Z) * X + x}

    ow_copy = pltpu.make_async_copy(ow_hbm, ow, ow_sem)
    ow_copy.start()
    barrier = pltpu.get_barrier_semaphore()

    def greet(delta, carry):
        pl.semaphore_signal(barrier, 1, device_id={"seg": lax.rem(me + delta, SEG)})
        return carry

    lax.fori_loop(1, SEG, greet, 0)

    for pair in range(SEG // 2):
        pieces = [
            q_ref[:, HEAD * (4 * pair + piece) : HEAD * (4 * pair + piece + 1)].astype(F32)
            for piece in range(4)
        ]
        qbuf[0, 16 * pair : 16 * pair + 16, :] = jnp.concatenate(pieces, axis=0).astype(BF16)
    qbuf[WINDOW] = jnp.zeros((2 * ROWS, HEAD), BF16)
    pl.semaphore_wait(barrier, SEG - 1)

    q_copies = []
    for slot in range(1, WINDOW):
        copy = pltpu.make_async_remote_copy(
            src_ref=qbuf.at[0],
            dst_ref=qbuf.at[slot],
            send_sem=q_ss.at[slot],
            recv_sem=q_rs.at[slot],
            device_id={"seg": lax.rem(me - slot + SEG, SEG)},
        )
        copy.start()
        q_copies.append(copy)

    aug[...] = jnp.zeros_like(aug)
    aug[0:SCORE, :] = resid_ref[...]
    closure_t = closure_transposed(par_ref[...])
    position_row = pos_ref[...]
    node_row = scored_nodes(node_ref[...], position_row)
    sub = iota((NODES, ROWS), 0)
    reach_t = mm(closure_t, hot(sub.astype(F32) == node_row)).astype(BF16)
    own_nodes = node_ref[pl.ds(me, 1), :]
    token_hot = jnp.where(sub == own_nodes, 1.0, 0.0).T.astype(BF16)
    linked = mm(token_hot, reach_t)
    visible = hot((linked > 0.5) & (sub + TOK * me <= position_row))
    wide_sub = iota((ROWS, 2 * ROWS), 0)
    wide_lane = iota((ROWS, 2 * ROWS), 1)
    wanted = lax.rem(SCORE * (me + wide_lane // 32) + lax.rem(wide_lane, SCORE), ROWS)
    mask = mm(visible, hot((wide_sub == wanted) & (wide_lane < 32 * WINDOW))) > 0.5

    for copy in q_copies:
        copy.wait_recv()

    scale = HEAD ** (-0.5)
    for k in range(KV_HEADS):
        query = qbuf[:, 32 * k : 32 * k + 32, :].reshape(2 * ROWS, HEAD)
        lanes = slice(HEAD * k, HEAD * k + HEAD)
        scores = jnp.where(mask, mm_nt(k_ref[:, lanes], query) * scale, NEGATIVE)
        top = jnp.max(scores, axis=0, keepdims=True)
        power = jnp.where(mask, jnp.exp(scores - top), 0.0)
        raised[k] = power
        parts[WINDOW - 1, k : k + 1, :] = top
        parts[WINDOW - 1, 8 + k : 9 + k, :] = jnp.sum(power, axis=0, keepdims=True)

    p_copies = []
    for delta in range(1, WINDOW):
        for way in (delta, -delta):
            copy = pltpu.make_async_remote_copy(
                src_ref=parts.at[WINDOW - 1],
                dst_ref=parts.at[WINDOW - 1 - way],
                send_sem=p_ss.at[WINDOW - 1 - way],
                recv_sem=p_rs.at[WINDOW - 1 - way],
                device_id={"seg": lax.rem(me + way + SEG, SEG)},
            )
            copy.start()
            p_copies.append(copy)
    for copy in p_copies:
        copy.wait_recv()
    part_slot = iota((8, 2 * ROWS), 1) // 32
    tops = []
    totals = []
    for away in range(1 - WINDOW, WINDOW):
        top = parts[away + WINDOW - 1, 0:8, :]
        total = parts[away + WINDOW - 1, 8:16, :]
        if away != 0:
            shift = (32 * away) % (2 * ROWS)
            top = pltpu.roll(top, shift, 1)
            total = pltpu.roll(total, shift, 1)
        valid = (part_slot >= away) & (part_slot < away + WINDOW)
        tops.append(jnp.where(valid, top, NEGATIVE))
        totals.append(jnp.where(valid, total, 0.0))
    peak = tops[0]
    for top in tops[1:]:
        peak = jnp.maximum(peak, top)
    whole = totals[0] * jnp.exp(tops[0] - peak)
    for top, total in zip(tops[1:], totals[1:]):
        whole = whole + total * jnp.exp(top - peak)
    factor = jnp.exp(parts[WINDOW - 1, 0:8, :] - peak) / jnp.where(whole > 0.0, whole, 1.0)
    for k in range(KV_HEADS):
        lanes = slice(HEAD * k, HEAD * k + HEAD)
        probs = raised[k] * factor[k : k + 1, :]
        mixed = mm(probs.T.astype(BF16), v_ref[:, lanes]).reshape(SLOTS, 4, 8, HEAD)
        for pair in range(4):
            osend[4 * k + pair] = mixed[0:WINDOW, pair].reshape(8 * WINDOW, HEAD)

    def o_copy(delta):
        there = lax.rem(me + delta, SEG)
        return pltpu.make_async_remote_copy(
            src_ref=osend.at[there],
            dst_ref=obuf.at[me],
            send_sem=o_ss.at[delta],
            recv_sem=o_rs.at[me],
            device_id={"seg": there},
        )

    def o_start(delta, carry):
        o_copy(delta).start()
        return carry

    lax.fori_loop(1, SEG, o_start, 0)
    obuf[me] = osend[me]

    def o_wait(delta, carry):
        source = lax.rem(me + delta, SEG)
        pltpu.make_async_remote_copy(
            src_ref=osend.at[source],
            dst_ref=obuf.at[source],
            send_sem=o_ss.at[delta],
            recv_sem=o_rs.at[source],
            device_id={"seg": source},
        ).wait_recv()
        return carry

    lax.fori_loop(1, SEG, o_wait, 0)

    sums = [None] * SEG
    for source in range(SEG):
        block = obuf[source]
        for slot in range(min(WINDOW, SEG - source)):
            row = source + slot
            term = block[8 * slot : 8 * slot + 8]
            sums[row] = term if sums[row] is None else sums[row] + term
    stacked = jnp.concatenate(sums, axis=0).astype(BF16)
    out_row = iota((2 * ROWS, 2 * ROWS), 0)
    in_row = iota((2 * ROWS, 2 * ROWS), 1)
    packed = lax.rem(out_row, ROWS)
    from_row = 8 * (packed // SCORE) + SCORE * (out_row // ROWS) + lax.rem(packed, SCORE)
    sorted_rows = mm(hot(in_row == from_row), stacked).astype(BF16)
    left = jnp.concatenate([sorted_rows[0:ROWS], sorted_rows[ROWS : 2 * ROWS]], axis=1)
    pick_row = iota((ROWS, 16), 0)
    pick_col = iota((ROWS, 16), 1)
    own_rows = hot((pick_row == SCORE * me + pick_col) & (pick_col < SCORE))

    def x_copy(delta, chunk):
        rows = pl.ds(pl.multiple_of(CROWS * lax.rem(chunk + z // 2, CHUNKS), CROWS), CROWS)
        return pltpu.make_async_remote_copy(
            src_ref=xsend.at[delta - 1, rows],
            dst_ref=xrecv.at[delta - 1, rows],
            send_sem=x_ss.at[delta - 1, chunk],
            recv_sem=x_rs.at[delta - 1, chunk],
            device_id=at_x(delta),
        )

    ow_copy.wait()
    for delta in (1, 3, 2, 0):
        cols = pl.ds(pl.multiple_of(DX * lax.rem(x + delta, X), DX), DX)
        product = mm(left, ow[:, cols]) + mm(own_rows, aug[:, cols])
        if delta == 0:
            xown[...] = product
        else:
            xsend[delta - 1] = encode(product)
            for chunk in range(CHUNKS):
                x_copy(delta, chunk).start()

    def z_copy(target, index):
        delta = lax.rem(target - z + Z, Z)
        return pltpu.make_async_remote_copy(
            src_ref=zsend.at[target],
            dst_ref=zrecv.at[delta],
            send_sem=z_ss.at[index],
            recv_sem=z_rs.at[delta],
            device_id={"seg": target * X + x},
        )

    for chunk in range(CHUNKS):
        for delta in (1, 3, 2):
            x_copy(delta, chunk).wait_recv()
        place = lax.rem(chunk + z // 2, CHUNKS)
        rows = pl.ds(pl.multiple_of(CROWS * place, CROWS), CROWS)
        total = xown[rows, :]
        for delta in (1, 3, 2):
            total = total + decode(xrecv[delta - 1, rows, :])
        for half in range(2):
            target = 2 * place + half
            piece = total[16 * half : 16 * half + 16]
            zsend[target] = encode(piece)

            @pl.when(target == z)
            def _():
                zown[...] = piece

            @pl.when(target != z)
            def _():
                z_copy(target, 2 * chunk + half).start()

    hidden = zown[...]
    for delta in range(1, Z):
        pltpu.make_async_remote_copy(
            src_ref=zsend.at[0],
            dst_ref=zrecv.at[delta],
            send_sem=z_ss.at[0],
            recv_sem=z_rs.at[delta],
            device_id=at_z(delta),
        ).wait_recv()
        hidden = hidden + decode(zrecv[delta])
    squares = jnp.sum(hidden * hidden, axis=1, keepdims=True)
    sqs[...] = jnp.broadcast_to(squares, sqs.shape)

    def s_copy(delta):
        return pltpu.make_async_remote_copy(
            src_ref=sqs,
            dst_ref=sqr.at[delta - 1],
            send_sem=s_ss.at[delta - 1],
            recv_sem=s_rs.at[delta - 1],
            device_id=at_x(delta),
        )

    for delta in range(1, X):
        s_copy(delta).start()
    gain = gain_ref[:, pl.ds(pl.multiple_of(DX * x, DX), DX)].astype(F32)
    for delta in range(1, X):
        s_copy(delta).wait_recv()
    power = (sqs[...] + sqr[0] + sqr[1] + sqr[2])[:, 0:1] / D
    normed_ref[...] = (hidden * lax.rsqrt(power + 1e-06) * gain).astype(BF16)

    for copy in q_copies + p_copies:
        copy.wait_send()

    def o_drain(delta, carry):
        o_copy(delta).wait_send()
        return carry

    lax.fori_loop(1, SEG, o_drain, 0)
    for delta in (1, 3, 2):
        for chunk in range(CHUNKS):
            x_copy(delta, chunk).wait_send()
    for chunk in range(CHUNKS):
        for half in range(2):
            target = 2 * lax.rem(chunk + z // 2, CHUNKS) + half

            @pl.when(target != z)
            def _():
                z_copy(target, 2 * chunk + half).wait_send()

    for delta in range(1, X):
        s_copy(delta).wait_send()


def encode(value):
    most = jnp.maximum(jnp.max(jnp.abs(value), axis=1, keepdims=True), 1e-30)
    level = jnp.ceil(jnp.log2(most * (1.0 / 32000.0)))
    scaled = jnp.round(value * jnp.exp2(-level)).astype(jnp.int32)
    levels = jnp.broadcast_to(level.astype(jnp.int32), (value.shape[0], HEAD))
    return jnp.concatenate([scaled, levels], axis=1).astype(jnp.int16)


def decode(code):
    wide = code.astype(jnp.int32).astype(F32)
    return wide[:, 0:DX] * jnp.exp2(wide[:, DX : DX + 1])


def vmem():
    return pl.BlockSpec(memory_space=pltpu.VMEM)


def attend(queries, keys, values, node_table, parents, positions, out_weight, resid, gain):
    sems = pltpu.SemaphoreType.DMA
    return pl.pallas_call(
        attend_body,
        out_shape=jax.ShapeDtypeStruct((16, DX), BF16),
        in_specs=[vmem()] * 6 + [pl.BlockSpec(memory_space=pl.ANY)] + [vmem()] * 2,
        out_specs=vmem(),
        scratch_shapes=[
            pltpu.VMEM((2 * HEAD, D), BF16),
            pltpu.VMEM((SLOTS, 2 * ROWS, HEAD), BF16),
            pltpu.VMEM((KV_HEADS, TOK, 2 * ROWS), F32),
            pltpu.VMEM((2 * WINDOW - 1, 16, 2 * ROWS), F32),
            pltpu.VMEM((SEG, 8 * WINDOW, HEAD), F32),
            pltpu.VMEM((SEG, 8 * WINDOW, HEAD), F32),
            pltpu.VMEM((16, D), BF16),
            pltpu.VMEM((X - 1, ROWS, DX + HEAD), jnp.int16),
            pltpu.VMEM((ROWS, DX), F32),
            pltpu.VMEM((X - 1, ROWS, DX + HEAD), jnp.int16),
            pltpu.VMEM((Z, 16, DX + HEAD), jnp.int16),
            pltpu.VMEM((16, DX), F32),
            pltpu.VMEM((Z, 16, DX + HEAD), jnp.int16),
            pltpu.VMEM((16, HEAD), F32),
            pltpu.VMEM((X - 1, 16, HEAD), F32),
            sems,
            sems((WINDOW,)),
            sems((WINDOW,)),
            sems((2 * WINDOW - 1,)),
            sems((2 * WINDOW - 1,)),
            sems((SEG,)),
            sems((SEG,)),
            sems((X - 1, CHUNKS)),
            sems((X - 1, CHUNKS)),
            sems((Z,)),
            sems((Z,)),
            sems((X - 1,)),
            sems((X - 1,)),
        ],
        compiler_params=pltpu.CompilerParams(
            collective_id=0, has_side_effects=True, vmem_limit_bytes=48 * MIB
        ),
    )(queries, keys, values, node_table, parents, positions, out_weight, resid, gain)


def merge_tiles(tiles):
    peak = tiles[0]
    for tile in tiles[1:]:
        peak = jnp.maximum(peak, tile)
    raised = jnp.exp(tiles[0] - peak)
    added = tiles[0]
    for tile in tiles[1:]:
        raised = raised + jnp.exp(tile - peak)
        added = added + tile
    return jnp.where(iota(peak.shape, 0) == 0, peak + jnp.log(raised), added)


def head_body(
    row_ref, w_hbm, node_ref, par_ref, pos_ref, leaf_ref, target_ref, old_ref, adv_ref,
    token_ref, leaf_out, loss_ref,
    w, part_a, part_b, part_c, logits, tiny, info, info_x, info_z, info_y,
    stat_s, stat_y, stat_x, stat_z, mine, mine_x, mine_z, last_s, last_r,
    w_sem, w_ss, w_rs, g_ss, g_rs, i_ss, i_rs, t_ss, t_rs, l_ss, l_rs,
):
    grp = lax.axis_index("grp")
    me = lax.axis_index("seg")
    y = grp // 2
    core = lax.rem(grp, 2)
    z = me // X
    x = lax.rem(me, X)
    at = {"x": x, "y": y, "z": z}
    size = {"x": X, "y": Y, "z": Z}

    def peer(axis, delta):
        moved = dict(at)
        moved[axis] = lax.rem(at[axis] + delta + size[axis], size[axis])
        return {"grp": moved["y"] * 2 + core, "seg": moved["z"] * X + moved["x"]}

    own_w = pltpu.make_async_copy(w_hbm, w.at[:, 0:VOC], w_sem)
    own_w.start()
    barrier = pltpu.get_barrier_semaphore()
    partners = [peer(axis, delta) for axis in "xyz" for delta in range(1, size[axis])]
    for delta in range(Y):
        partners.append({"grp": lax.rem(y + delta, Y) * 2 + 1 - core, "seg": me})
    for partner in partners:
        pl.semaphore_signal(barrier, 1, device_id=partner)

    bufs = (part_a, part_b, part_c)
    for (offset, width, order), buf in zip(PARTS, bufs):
        buf[x, y, z] = row_ref[:, offset : offset + width]
    tile_sub = iota((8, ROWS), 0)
    tile_lane = iota((8, ROWS), 1)
    tiny[...] = jnp.zeros_like(tiny)
    tiny[0:1, 0:SCORE] = target_ref[...].astype(F32)
    tiny[1:2, 0:SCORE] = old_ref[...]
    tiny[2:3, 0:2] = adv_ref[...]
    start = tiny[...]
    info[...] = jnp.where(
        tile_sub < 2, pltpu.roll(start, SCORE * me, 1), pltpu.roll(start, 2 * me, 1)
    )
    pl.semaphore_wait(barrier, len(partners))

    pending = []
    swap = pltpu.make_async_remote_copy(
        src_ref=w_hbm,
        dst_ref=w.at[:, VOC : 2 * VOC],
        send_sem=w_ss,
        recv_sem=w_rs,
        device_id={"grp": y * 2 + 1 - core, "seg": me},
    )

    def spread(axis, sources, into, base, ss, rs):
        count = size[axis]
        here = at[axis]
        for delta in range(1, count):
            there = lax.rem(here + delta, count)
            copy = pltpu.make_async_remote_copy(
                src_ref=sources(there),
                dst_ref=into.at[here],
                send_sem=ss.at[base + delta],
                recv_sem=rs.at[base + here],
                device_id=peer(axis, delta),
            )
            copy.start()
            pending.append(copy)

    def collect(axis, into, base, ss, rs):
        count = size[axis]
        here = at[axis]
        for delta in range(1, count):
            there = lax.rem(here + delta, count)
            pltpu.make_async_remote_copy(
                src_ref=into.at[there],
                dst_ref=into.at[there],
                send_sem=ss.at[base + delta],
                recv_sem=rs.at[base + there],
                device_id=peer(axis, delta),
            ).wait_recv()

    def gather(part, buf, order):
        ready = []
        for stage, axis in enumerate(order):
            count = size[axis]
            done = order[:stage]

            def block(index, half):
                where = []
                for name in "xyz":
                    if name == axis:
                        where.append(lax.rem(index + 2 * count, count))
                    elif name not in done:
                        where.append(at[name])
                    elif half is not None and name == done[0]:
                        cut = size[name] // 2
                        where.append(pl.ds(half * cut, cut))
                    else:
                        where.append(slice(None))
                return buf.at[tuple(where)]

            def ring(step, way):
                half = None
                if step == count // 2:
                    if stage == 0:
                        if way < 0:
                            return None
                    else:
                        half = 0 if way > 0 else 1
                index = ((part * 3 + stage) * 4 + step - 1) * 2 + (way < 0)
                sent = block(at[axis] - way * (step - 1), half)
                landed = block(at[axis] - way * step, half)
                send = pltpu.make_async_remote_copy(
                    src_ref=sent,
                    dst_ref=sent,
                    send_sem=g_ss.at[index],
                    recv_sem=g_rs.at[index],
                    device_id=peer(axis, way),
                )
                arrive = pltpu.make_async_remote_copy(
                    src_ref=landed,
                    dst_ref=landed,
                    send_sem=g_ss.at[index],
                    recv_sem=g_rs.at[index],
                    device_id=peer(axis, way),
                )
                return send, arrive

            for step in range(1, count // 2 + 1):
                for copy in ready:
                    copy.wait_recv()
                ready = []
                for way in (1, -1):
                    both = ring(step, way)
                    if both is not None:
                        both[0].start()
                        pending.append(both[0])
                        ready.append(both[1])
                yield
        for copy in ready:
            copy.wait_recv()

    def tell():
        info_x[x] = info[...]
        spread("x", lambda there: info_x.at[x], info_x, 0, i_ss, i_rs)
        yield
        yield
        collect("x", info_x, 0, i_ss, i_rs)
        info_z[z] = info_x[0] + info_x[1] + info_x[2] + info_x[3]
        spread("z", lambda there: info_z.at[z], info_z, X, i_ss, i_rs)
        yield
        yield
        collect("z", info_z, X, i_ss, i_rs)
        whole = info_z[0]
        for index in range(1, Z):
            whole = whole + info_z[index]
        info_y[y] = whole
        spread("y", lambda there: info_y.at[y], info_y, X + Z, i_ss, i_rs)
        yield
        yield
        collect("y", info_y, X + Z, i_ss, i_rs)

    running = [
        gather(part, buf, order) for part, ((offset, width, order), buf) in enumerate(zip(PARTS, bufs))
    ]
    running.append(tell())
    first = True
    while running:
        for item in list(running):
            try:
                next(item)
            except StopIteration:
                running.remove(item)
        if first:
            swap.start()
            first = False

    own_w.wait()
    swap.wait_recv()

    def columns(n, carry):
        cols = pl.ds(pl.multiple_of(256 * n, 256), 256)
        total = None
        for (offset, width, order), buf in zip(PARTS, bufs):
            for index in range(X):
                rows = buf[index].reshape(Y * Z * 16, width)
                term = mm(rows, w[DX * index + offset : DX * index + offset + width, cols])
                total = term if total is None else total + term
        logits[:, cols] = total
        return carry

    lax.fori_loop(0, 2 * VOC // 256, columns, 0)

    voc_lane = iota((ROWS, 2 * VOC), 1)
    own_base = (grp * SEG + me) * VOC
    other_base = ((2 * y + 1 - core) * SEG + me) * VOC - VOC
    voc_id = (voc_lane + jnp.where(voc_lane < VOC, own_base, other_base)).astype(F32)
    targets = jnp.concatenate(
        [info_y[...].reshape(8 * Y, ROWS), jnp.zeros((ROWS - 8 * Y, ROWS), F32)], axis=0
    ).T
    square_lane = iota((ROWS, ROWS), 1)
    for index in range(Y):
        block = logits[ROWS * index : ROWS * index + ROWS, :]
        top = jnp.max(block, axis=1, keepdims=True)
        lse = top + jnp.log(jnp.sum(jnp.exp(block - top), axis=1, keepdims=True))
        found = voc_id == targets[:, 8 * index : 8 * index + 1]
        picked = jnp.sum(jnp.where(found, block, 0.0), axis=1, keepdims=True)
        both = jnp.where(square_lane == 0, lse, jnp.where(square_lane == 1, picked, 0.0))
        stat_s[index] = both.T[0:8]
    spread("y", lambda there: stat_s.at[there], stat_y, 0, t_ss, t_rs)
    stat_y[y] = stat_s[y]

    closure_t = closure_transposed(par_ref[...])
    node_row = scored_nodes(node_ref[...], pos_ref[...])
    sub = iota((NODES, ROWS), 0)
    row_hot_t = hot(sub.astype(F32) == node_row)
    leaf_sub = iota((NODES, LEAVES), 0)
    leaf_hot_t = hot(leaf_sub == leaf_ref[...])
    leaf_reach_t = mm(closure_t, leaf_hot_t)
    leaf_reach = jnp.concatenate([leaf_reach_t, jnp.zeros((NODES, NODES - LEAVES), F32)], axis=1).T
    path = mm(leaf_reach.astype(BF16), row_hot_t)
    counts = jnp.maximum(jnp.sum(path, axis=1, keepdims=True), 1.0)

    collect("y", stat_y, 0, t_ss, t_rs)
    mine[...] = merge_tiles([stat_y[index] for index in range(Y)])
    spread("x", lambda there: mine, stat_x, Y, t_ss, t_rs)
    stat_x[x] = mine[...]
    collect("x", stat_x, Y, t_ss, t_rs)
    mine_x[...] = merge_tiles([stat_x[index] for index in range(X)])
    spread("z", lambda there: mine_x, stat_z, Y + X, t_ss, t_rs)
    stat_z[z] = mine_x[...]
    collect("z", stat_z, Y + X, t_ss, t_rs)
    merged = merge_tiles([stat_z[index] for index in range(Z)])

    own_info = info_y[y]
    token_row = merged[1:2] - merged[0:1] - own_info[1:2]
    shift = lax.rem(ROWS - SCORE * me, ROWS)
    token_ref[...] = pltpu.roll(jnp.broadcast_to(token_row, (8, ROWS)), shift, 1)[0:1, 0:SCORE]
    means = jnp.sum(path * token_row, axis=1, keepdims=True) / counts
    leaf_row = jnp.broadcast_to(means, (ROWS, ROWS)).T[0:8]
    leaf_out[...] = pltpu.roll(leaf_row, lax.rem(ROWS - 2 * me, ROWS), 1)[0:1, 0:2]
    gains = own_info[2:3]
    ratio = jnp.exp(leaf_row)
    terms = jnp.minimum(ratio * gains, jnp.clip(ratio, 1.0 - EPS_LOW, 1.0 + EPS_HIGH) * gains)
    terms = jnp.where((tile_sub == 0) & (tile_lane < LEAVES), terms, 0.0)
    last_s[...] = terms

    last = []
    for delta in range(1, GRP):
        copy = pltpu.make_async_remote_copy(
            src_ref=last_s,
            dst_ref=last_r.at[grp],
            send_sem=l_ss.at[delta],
            recv_sem=l_rs.at[grp],
            device_id={"grp": lax.rem(grp + delta, GRP), "seg": me},
        )
        copy.start()
        last.append(copy)
    last_r[grp] = terms
    for delta in range(1, GRP):
        there = lax.rem(grp + delta, GRP)
        pltpu.make_async_remote_copy(
            src_ref=last_s,
            dst_ref=last_r.at[there],
            send_sem=l_ss.at[delta],
            recv_sem=l_rs.at[there],
            device_id={"grp": there, "seg": me},
        ).wait_recv()
    everything = last_r[0]
    for index in range(1, GRP):
        everything = everything + last_r[index]
    loss_ref[...] = -jnp.sum(everything, axis=(0, 1), keepdims=True) / (LEAVES * GRP)

    for copy in pending:
        copy.wait_send()
    swap.wait_send()
    for copy in last:
        copy.wait_send()


def head(rows, vocab_weight, node_table, parents, positions, leaf_node, targets, old_logp, advantages):
    sems = pltpu.SemaphoreType.DMA
    tile = pltpu.VMEM((8, ROWS), F32)

    def tiles(count):
        return pltpu.VMEM((count, 8, ROWS), F32)

    return pl.pallas_call(
        head_body,
        out_shape=(
            jax.ShapeDtypeStruct((1, SCORE), F32),
            jax.ShapeDtypeStruct((1, 2), F32),
            jax.ShapeDtypeStruct((1, 1), F32),
        ),
        in_specs=[vmem(), pl.BlockSpec(memory_space=pl.ANY)] + [vmem()] * 7,
        out_specs=(vmem(), vmem(), vmem()),
        scratch_shapes=[pltpu.VMEM((D, 2 * VOC), BF16)]
        + [pltpu.VMEM((X, Y, Z, 16, width), BF16) for offset, width, order in PARTS]
        + [
            pltpu.VMEM((Y * ROWS, 2 * VOC), F32),
            tile,
            tile,
            tiles(X),
            tiles(Z),
            tiles(Y),
            tiles(Y),
            tiles(Y),
            tiles(X),
            tiles(Z),
            tile,
            tile,
            tile,
            tile,
            tiles(GRP),
            sems,
            sems,
            sems,
            sems((72,)),
            sems((72,)),
            sems((X + Y + Z,)),
            sems((X + Y + Z,)),
            sems((X + Y + Z,)),
            sems((X + Y + Z,)),
            sems((GRP,)),
            sems((GRP,)),
        ],
        compiler_params=pltpu.CompilerParams(
            collective_id=1, has_side_effects=True, vmem_limit_bytes=56 * MIB
        ),
    )(rows, vocab_weight, node_table, parents, positions, leaf_node, targets, old_logp, advantages)


def body(
    queries, keys, values, node_ids, parents, score_pos, out_weight, resid, norm_gain,
    vocab_weight, targets, old_logp, leaf_node, advantages,
):
    node_table = node_ids.reshape(SEG, TOK)
    rows = attend(
        queries[0], keys[0], values[0], node_table, parents, score_pos, out_weight, resid[0],
        norm_gain.reshape(1, D),
    )
    token, leaf, loss = head(
        rows, vocab_weight, node_table, parents, score_pos, leaf_node, targets, old_logp, advantages
    )
    return (token, leaf, loss.reshape(()))


def solution(mesh):
    placed = (
        P("grp", "seg", None),
        P("grp", "seg", None),
        P("grp", "seg", None),
        P("grp", None),
        P("grp", None),
        P("grp", None),
        P("seg", None),
        P("grp", "seg", None),
        P(),
        P(None, ("grp", "seg")),
        P("grp", "seg"),
        P("grp", "seg"),
        P("grp", None),
        P("grp", "seg"),
    )
    return jax.shard_map(
        body,
        mesh=mesh,
        in_specs=placed,
        out_specs=(P("grp", "seg"), P("grp", "seg"), P()),
        check_vma=False,
    )
```

profile of v0, /device:TPU:1, one launch (start us, length us, event | category | flops | bytes accessed | tf_op | source)
XLA Modules:
  0.0 167.3 jit_solution(8338953347659233180)
XLA Ops:
  0.6 0.7 reshape.16.gain_ref
  1.3 0.0 copy-start
  1.4 1.7 %copy-done = bf16[256,5120]{1,0:T(8,128)(2,1)S(1)} copy-done((bf16[256,5120]{1,0:T(8,128)(2,1)S(1)}, bf16[256,5120]{1,0:T(8,128)(2,1)}, u32[]{:S(2)}) %copy-start) | copy-done | bytes 2621464
  3.1 0.0 copy-start.1
  3.1 0.9 copy-done.1
  4.0 0.0 copy-start.2
  4.0 0.9 copy-done.2
  5.0 0.0 copy-start.4
  5.0 0.7 copy-done.4
  5.7 0.0 copy-start.5
  5.7 0.8 copy-done.5
  6.6 0.0 copy-start.6
  6.6 0.8 copy-done.6
  7.3 0.0 copy-start.7
  7.3 0.7 copy-done.7
  8.0 0.0 copy-start.8
  8.0 0.7 copy-done.8
  8.6 76.7 %shard_map.157.row_ref = bf16[16,1280]{1,0:T(8,128)(2,1)S(1)} custom-call(bf16[4,8192]{1,0:T(4,128)(2,1)S(1)} %bitcast.10, bf16[128,1024]{1,0:T(8,128)(2,1)S(1)} %bitcast.6, bf16[128,1024]{1,0:T(8,128)(2,1)S(1)} %bitcast.7, s32[32,128]{1,0:T(8,128)S(1)} %bitcast.9, s32[1,128]{1,0:T(1,128)S(1)} %copy-done.7, s32[1,128]{1,0:T(1,128)S(1)} %copy-done.8, ...), custom_call_target="tpu_custom_call" | custom-call | tf_op jit(solution)/shard_map/pallas_call | solution.py:360
  85.3 0.0 copy-start.3
  85.3 0.6 copy-done.3
  85.9 77.4 %shard_map.158 = (f32[1,4]{1,0:T(1,128)}, f32[1,2]{1,0:T(1,128)}, f32[1,1]{1,0:T(1,128)}) custom-call(bf16[16,1280]{1,0:T(8,128)(2,1)} %copy-done.3, bf16[5120,384]{1,0:T(8,128)(2,1)} %w_hbm.1, s32[32,128]{1,0:T(8,128)} %bitcast.8, s32[1,128]{1,0:T(1,128)} %par_ref.3, s32[1,128]{1,0:T(1,128)} %pos_ref.3, s32[1,64]{1,0:T(1,128)} %leaf_ref.1, ...), custom_call_target="tpu_custom_call" | custom-call | tf_op jit(solution)/shard_map/pallas_call | solution.py:701
  163.3 1.1 copy.20
  164.4 1.1 copy.21
Async XLA Ops:
  1.3 1.7 %copy-start = (bf16[256,5120]{1,0:T(8,128)(2,1)S(1)}, bf16[256,5120]{1,0:T(8,128)(2,1)}, u32[]{:S(2)}) copy-start(bf16[256,5120]{1,0:T(8,128)(2,1)} %ow_hbm.1) | copy-start | bytes 7864324
  3.1 0.9 copy-start.1
  4.0 0.9 copy-start.2
  5.0 0.7 copy-start.4
  5.7 0.8 copy-start.5
  6.6 0.8 copy-start.6
  7.3 0.7 copy-start.7
  8.0 0.7 copy-start.8
  85.3 0.6 copy-start.3
where the time goes:
time: 168 us; the launch traced here: 167 us
  Pallas kernels  154 us (92%)
  local copies, waits for them, and re-layouts  10.8 us (6%)
  between operations  2.43 us (1%)
    pallas_call x1, Pallas kernels, head(): pl.pallas_call(head_body, out_shape=(jax.ShapeDtypeStruct((1, SCORE), F32...  77.4 us
    pallas_call x1, Pallas kernels, attend(): pl.pallas_call(attend_body, out_shape=jax.ShapeDtypeStruct((16, DX), BF16...  76.7 us
    unnamed x20, local copies, waits for them, and re-layouts  10.1 us

commit v1 on v0

v1 whole, which is shorter than its diff:
```python
import jax
import jax.numpy as jnp
from jax import lax
from jax.experimental import pallas as pl
from jax.experimental.pallas import tpu as pltpu
from jax.sharding import PartitionSpec as P

F32 = jnp.float32
BF16 = jnp.bfloat16
EPS_LOW = 0.0003
EPS_HIGH = 0.0004
NEGATIVE = -1e30
HEAD = 128
KV_HEADS = 8
X, Y, Z = 4, 4, 8
SEG = X * Z
GRP = 2 * Y
TOK = 128
ROWS = 128
NODES = 128
LEAVES = 64
SCORE = 4
WINDOW = 7
SLOTS = 8
OWNERS = X - 1 + WINDOW
D = 5120
DX = D // X
VOC = 384
PARTS = ((0, 512, "xyz"), (512, 384, "yzx"), (896, 384, "zxy"))
MIB = 1024 * 1024


def iota(shape, dim):
    return lax.broadcasted_iota(jnp.int32, shape, dim)


def hot(mask):
    return mask.astype(F32).astype(BF16)


def mm(a, b):
    return jnp.dot(a, b, preferred_element_type=F32)


def mm_nt(a, b):
    return lax.dot_general(a, b, (((1,), (1,)), ((), ())), preferred_element_type=F32)


def closure_transposed(parent_row):
    sub = iota((NODES, NODES), 0)
    lane = iota((NODES, NODES), 1)
    step = jnp.where((sub == parent_row) | (sub == lane), 1.0, 0.0)
    for squaring in range(3):
        half = step.astype(BF16)
        step = jnp.minimum(mm(half, half), 1.0)
    return step.astype(BF16)


def scored_nodes(node_table, position_row):
    table = jnp.concatenate([node_table.astype(F32), jnp.zeros((TOK - SEG, TOK), F32)], axis=0)
    across = table.T.astype(BF16)
    sub = iota((TOK, ROWS), 0)
    lane = iota((TOK, ROWS), 1)
    spread = mm(across, hot(sub == lane // SCORE))
    match = sub == position_row - TOK * (lane // SCORE)
    return jnp.sum(jnp.where(match, spread, 0.0), axis=0, keepdims=True)


def front(
    me, grp, q_ref, k_ref, v_ref, node_ref, par_ref, pos_ref, ow_hbm, resid_ref, gain_ref,
    qbuf, raised, parts, factors, osend, oxr, ozs, ozr, mixs, mixr, wown, wx, rsend, rrecv,
    zsend, zown, zrecv, sqs, sqr,
    w_sem, q_ss, q_rs, p_ss, p_rs, ox_ss, ox_rs, oz_ss, oz_rs, m_ss, m_rs, wx_ss, wx_rs, wy_ss, wy_rs,
    r_ss, r_rs, z_ss, z_rs, s_ss, s_rs, greet, early, middle,
):
    z = me // X
    x = lax.rem(me, X)
    pending = []

    def at_x(delta):
        return {"seg": z * X + lax.rem(x + delta, X)}

    def at_z(delta):
        return {"seg": lax.rem(z + delta, Z) * X + x}

    def send(src, dst, ss, rs, device):
        copy = pltpu.make_async_remote_copy(
            src_ref=src, dst_ref=dst, send_sem=ss, recv_sem=rs, device_id=device
        )
        copy.start()
        pending.append(copy)

    def landed(dst, ss, rs, device):
        pltpu.make_async_remote_copy(
            src_ref=dst, dst_ref=dst, send_sem=ss, recv_sem=rs, device_id=device
        ).wait_recv()

    def dx_cols(at):
        return pl.ds(pl.multiple_of(DX * at, DX), DX)

    own_weight = pltpu.make_async_copy(ow_hbm.at[:, dx_cols(x)], wown, w_sem)
    own_weight.start()
    for pair in range(SEG // 2):
        spot = []
        for half in range(2):
            h = 2 * pair + half
            spot += [
                q_ref[:, HEAD * (2 * h + piece) : HEAD * (2 * h + piece + 1)].astype(F32)
                for piece in range(2)
            ]
        k = pair // 2
        row = HEAD * (k % 2) + 32 * (k // 2) + 16 * (pair % 2)
        qbuf[0, row : row + 16, :] = jnp.concatenate(spot, axis=0).astype(BF16)
    qbuf[WINDOW] = jnp.zeros((2 * ROWS, HEAD), BF16)
    greet()

    for c in range(2):
        rows = pl.ds(HEAD * c, HEAD)
        for slot in range(1, WINDOW):
            send(
                qbuf.at[0, rows],
                qbuf.at[slot, rows],
                q_ss.at[c, slot],
                q_rs.at[c, slot],
                {"seg": lax.rem(me - slot + SEG, SEG)},
            )

    slab = pl.ds(pl.multiple_of(32 * grp, 32), 32)
    for delta in range(1, X):
        send(
            ow_hbm.at[slab, dx_cols(lax.rem(x + delta, X))],
            wx.at[delta - 1, slab],
            wx_ss.at[delta - 1],
            wx_rs.at[delta - 1],
            at_x(delta),
        )
    early()

    place_row = iota((16, 16), 0)
    place_col = iota((16, 16), 1)
    place = hot((place_row == SCORE * x + place_col) & (place_col < SCORE))
    for delta in range(X):
        cols = resid_ref[:, dx_cols(lax.rem(x + delta, X))]
        padded = jnp.concatenate([cols.astype(F32), jnp.zeros((16 - SCORE, DX), F32)], axis=0)
        rsend[delta] = mm(place, padded.astype(BF16)).astype(BF16)
        if delta:
            send(rsend.at[delta], rrecv.at[delta - 1], r_ss.at[delta], r_rs.at[delta], at_x(delta))

    closure_t = closure_transposed(par_ref[...])
    position_row = pos_ref[...]
    node_row = scored_nodes(node_ref[...], position_row)
    sub = iota((NODES, ROWS), 0)
    row_hot_t = hot(sub.astype(F32) == node_row)
    reach_t = mm(closure_t, row_hot_t).astype(BF16)
    own_nodes = node_ref[pl.ds(me, 1), :]
    token_hot = jnp.where(sub == own_nodes, 1.0, 0.0).T.astype(BF16)
    linked = mm(token_hot, reach_t)
    visible = hot((linked > 0.5) & (sub + TOK * me <= position_row))
    wide_sub = iota((ROWS, 2 * ROWS), 0)
    wide_lane = iota((ROWS, 2 * ROWS), 1)
    wanted = lax.rem(SCORE * (me + wide_lane // 32) + lax.rem(wide_lane, SCORE), ROWS)
    mask = mm(visible, hot((wide_sub == wanted) & (wide_lane < 32 * WINDOW))) > 0.5

    scale = HEAD ** (-0.5)
    for c in range(2):
        for slot in range(1, WINDOW):
            landed(
                qbuf.at[slot, pl.ds(HEAD * c, HEAD)],
                q_ss.at[c, slot],
                q_rs.at[c, slot],
                {"seg": lax.rem(me + slot, SEG)},
            )
        for i in range(4):
            k = 2 * i + c
            row = HEAD * c + 32 * i
            query = qbuf[:, row : row + 32, :].reshape(2 * ROWS, HEAD)
            lanes = slice(HEAD * k, HEAD * k + HEAD)
            scores = jnp.where(mask, mm_nt(k_ref[:, lanes], query) * scale, NEGATIVE)
            top = jnp.max(scores, axis=0, keepdims=True)
            power = jnp.where(mask, jnp.exp(scores - top), 0.0)
            raised[4 * c + i] = power
            parts[c, WINDOW - 1, i : i + 1, :] = top
            parts[c, WINDOW - 1, 4 + i : 5 + i, :] = jnp.sum(power, axis=0, keepdims=True)
        for delta in range(1, WINDOW):
            for way in (delta, -delta):
                slot = WINDOW - 1 - way
                send(
                    parts.at[c, WINDOW - 1],
                    parts.at[c, slot],
                    p_ss.at[c, slot],
                    p_rs.at[c, slot],
                    {"seg": lax.rem(me + way + SEG, SEG)},
                )

    for delta in range(1, X):
        landed(wx.at[delta - 1, slab], wx_ss.at[delta - 1], wx_rs.at[delta - 1], at_x(delta))
    for delta in range(1, GRP):
        send(
            wx.at[:, slab],
            wx.at[:, slab],
            wy_ss.at[delta],
            wy_rs.at[grp],
            {"grp": lax.rem(grp + delta, GRP), "seg": me},
        )

    part_slot = iota((4, 2 * ROWS), 1) // 32
    for c in range(2):
        tops = []
        totals = []
        for away in range(1 - WINDOW, WINDOW):
            slot = away + WINDOW - 1
            if away != 0:
                landed(
                    parts.at[c, slot],
                    p_ss.at[c, slot],
                    p_rs.at[c, slot],
                    {"seg": lax.rem(me + away + SEG, SEG)},
                )
            value = parts[c, slot]
            if away != 0:
                value = pltpu.roll(value, (32 * away) % (2 * ROWS), 1)
            valid = (part_slot >= away) & (part_slot < away + WINDOW)
            tops.append(jnp.where(valid, value[0:4], NEGATIVE))
            totals.append(jnp.where(valid, value[4:8], 0.0))
        peak = tops[0]
        for top in tops[1:]:
            peak = jnp.maximum(peak, top)
        whole = totals[0] * jnp.exp(tops[0] - peak)
        for top, total in zip(tops[1:], totals[1:]):
            whole = whole + total * jnp.exp(top - peak)
        own_top = parts[c, WINDOW - 1][0:4]
        factors[c, 0:4, :] = jnp.exp(own_top - peak) / jnp.where(whole > 0.0, whole, 1.0)
        for step in range(4):
            i = lax.rem(z // 2 + step, 4)
            at = 4 * c + i
            lanes = pl.ds(pl.multiple_of(HEAD * (2 * i + c), HEAD), HEAD)
            probs = raised[at] * factors[c, pl.ds(i, 1), :]
            mixed = mm(probs.T.astype(BF16), v_ref[:, lanes]).reshape(SLOTS, 4, 8, HEAD)
            for pair in range(4):
                osend[at, pair] = mixed[0:WINDOW, pair].reshape(8 * WINDOW, HEAD)
            for delta in (1, 3, 2):
                send(
                    osend.at[at, lax.rem(x + delta, X)],
                    oxr.at[at, delta - 1],
                    ox_ss.at[4 * c + step, delta - 1],
                    ox_rs.at[at, delta - 1],
                    at_x(delta),
                )

    guarded = []
    for c in range(2):
        for step in range(4):
            i = lax.rem(z // 2 + step, 4)
            at = 4 * c + i
            target = 2 * i + c
            for delta in (1, 3, 2):
                landed(
                    oxr.at[at, delta - 1],
                    ox_ss.at[4 * c + step, delta - 1],
                    ox_rs.at[at, delta - 1],
                    at_x(delta),
                )
            ozs[at] = jnp.zeros((8 * OWNERS, HEAD), F32)
            ozs[at, pl.ds(pl.multiple_of(8 * x, 8), 8 * WINDOW), :] = osend[at, x]
            for delta in range(1, X):
                span = pl.ds(pl.multiple_of(8 * lax.rem(x - delta + X, X), 8), 8 * WINDOW)
                ozs[at, span, :] = ozs[at, span, :] + oxr[at, delta - 1]
            away_copy = pltpu.make_async_remote_copy(
                src_ref=ozs.at[at],
                dst_ref=ozr.at[z],
                send_sem=oz_ss.at[4 * c + step],
                recv_sem=oz_rs.at[z],
                device_id={"seg": target * X + x},
            )
            if step == 0:
                guarded.append((target, away_copy))

                @pl.when(target == z)
                def _():
                    ozr[z] = ozs[at]

                @pl.when(target != z)
                def _():
                    away_copy.start()

            else:
                away_copy.start()
                pending.append(away_copy)

    middle(closure_t, row_hot_t)

    for delta in range(1, Z):
        source = lax.rem(z + delta, Z)
        landed(ozr.at[source], oz_ss.at[0], oz_rs.at[source], at_z(delta))
    sums = [None] * SEG
    for source in range(Z):
        block = ozr[source]
        for slot in range(OWNERS):
            row = X * source + slot
            if row < SEG:
                term = block[8 * slot : 8 * slot + 8]
                sums[row] = term if sums[row] is None else sums[row] + term
    stacked = jnp.concatenate(sums, axis=0).astype(BF16)
    out_row = iota((2 * ROWS, 2 * ROWS), 0)
    in_row = iota((2 * ROWS, 2 * ROWS), 1)
    packed = lax.rem(out_row, ROWS)
    from_row = 8 * (packed // SCORE) + SCORE * (out_row // ROWS) + lax.rem(packed, SCORE)
    sorted_rows = mm(hot(in_row == from_row), stacked).astype(BF16)
    left = jnp.concatenate([sorted_rows[0:ROWS], sorted_rows[ROWS : 2 * ROWS]], axis=1)
    mixs[...] = left
    for delta in (1, 3, 2):
        send(mixs, mixr.at[delta - 1], m_ss.at[delta - 1], m_rs.at[delta - 1], at_x(delta))
    own_weight.wait()
    product = mm(left, wown[...])
    for delta in range(1, GRP):
        other = lax.rem(grp + delta, GRP)
        theirs = pl.ds(pl.multiple_of(32 * other, 32), 32)
        landed(wx.at[:, theirs], wy_ss.at[delta], wy_rs.at[other], {"grp": other, "seg": me})
    for delta in (1, 3, 2):
        landed(mixr.at[delta - 1], m_ss.at[delta - 1], m_rs.at[delta - 1], at_x(delta))
        product = product + mm(mixr[delta - 1], wx[delta - 1])
    zown[...] = product

    for delta in (1, 7, 2, 6, 3, 5, 4):
        target = lax.rem(z + delta, Z)
        zsend[delta] = encode(zown[pl.ds(pl.multiple_of(16 * target, 16), 16), :])
        send(zsend.at[delta], zrecv.at[delta], z_ss.at[delta], z_rs.at[delta], at_z(delta))
    hidden = zown[pl.ds(pl.multiple_of(16 * z, 16), 16), :] + rsend[0].astype(F32)
    for delta in range(1, X):
        landed(rrecv.at[delta - 1], r_ss.at[delta], r_rs.at[delta], at_x(delta))
        hidden = hidden + rrecv[delta - 1].astype(F32)
    for delta in (1, 7, 2, 6, 3, 5, 4):
        landed(zrecv.at[delta], z_ss.at[delta], z_rs.at[delta], at_z(delta))
        hidden = hidden + decode(zrecv[delta])
    squares = jnp.sum(hidden * hidden, axis=1, keepdims=True)
    sqs[...] = jnp.broadcast_to(squares, sqs.shape)
    for delta in (1, 3, 2):
        send(sqs, sqr.at[delta - 1], s_ss.at[delta - 1], s_rs.at[delta - 1], at_x(delta))
    gain = gain_ref[:, dx_cols(x)].astype(F32)
    for delta in (1, 3, 2):
        landed(sqr.at[delta - 1], s_ss.at[delta - 1], s_rs.at[delta - 1], at_x(delta))
    power = (sqs[...] + sqr[0] + sqr[1] + sqr[2])[:, 0:1] / D
    normed = (hidden * lax.rsqrt(power + 1e-06) * gain).astype(BF16)

    def drain():
        for copy in pending:
            copy.wait_send()
        for target, copy in guarded:

            @pl.when(target != z)
            def _():
                copy.wait_send()

    return normed, drain


def front_scratch():
    sems = pltpu.SemaphoreType.DMA
    return [
        pltpu.VMEM((SLOTS, 2 * ROWS, HEAD), BF16),
        pltpu.VMEM((KV_HEADS, TOK, 2 * ROWS), F32),
        pltpu.VMEM((2, 2 * WINDOW - 1, 8, 2 * ROWS), F32),
        pltpu.VMEM((2, 8, 2 * ROWS), F32),
        pltpu.VMEM((KV_HEADS, X, 8 * WINDOW, HEAD), F32),
        pltpu.VMEM((KV_HEADS, X - 1, 8 * WINDOW, HEAD), F32),
        pltpu.VMEM((KV_HEADS, 8 * OWNERS, HEAD), F32),
        pltpu.VMEM((Z, 8 * OWNERS, HEAD), F32),
        pltpu.VMEM((ROWS, 2 * HEAD), BF16),
        pltpu.VMEM((X - 1, ROWS, 2 * HEAD), BF16),
        pltpu.VMEM((2 * HEAD, DX), BF16),
        pltpu.VMEM((X - 1, 2 * HEAD, DX), BF16),
        pltpu.VMEM((X, 16, DX), BF16),
        pltpu.VMEM((X - 1, 16, DX), BF16),
        pltpu.VMEM((Z, 16, DX + HEAD), jnp.int16),
        pltpu.VMEM((ROWS, DX), F32),
        pltpu.VMEM((Z, 16, DX + HEAD), jnp.int16),
        pltpu.VMEM((16, HEAD), F32),
        pltpu.VMEM((X - 1, 16, HEAD), F32),
        sems,
        sems((2, WINDOW)),
        sems((2, WINDOW)),
        sems((2, 2 * WINDOW - 1)),
        sems((2, 2 * WINDOW - 1)),
        sems((KV_HEADS, X - 1)),
        sems((KV_HEADS, X - 1)),
        sems((Z,)),
        sems((Z,)),
        sems((X - 1,)),
        sems((X - 1,)),
        sems((X - 1,)),
        sems((X - 1,)),
        sems((GRP,)),
        sems((GRP,)),
        sems((X,)),
        sems((X,)),
        sems((Z,)),
        sems((Z,)),
        sems((X - 1,)),
        sems((X - 1,)),
    ]


def encode(value):
    most = jnp.maximum(jnp.max(jnp.abs(value), axis=1, keepdims=True), 1e-30)
    level = jnp.ceil(jnp.log2(most * (1.0 / 32000.0)))
    scaled = jnp.round(value * jnp.exp2(-level)).astype(jnp.int32)
    levels = jnp.broadcast_to(level.astype(jnp.int32), (value.shape[0], HEAD))
    return jnp.concatenate([scaled, levels], axis=1).astype(jnp.int16)


def decode(code):
    wide = code.astype(jnp.int32).astype(F32)
    return wide[:, 0:DX] * jnp.exp2(wide[:, DX : DX + 1])


def vmem():
    return pl.BlockSpec(memory_space=pltpu.VMEM)


def merge_tiles(tiles):
    peak = tiles[0]
    for tile in tiles[1:]:
        peak = jnp.maximum(peak, tile)
    raised = jnp.exp(tiles[0] - peak)
    added = tiles[0]
    for tile in tiles[1:]:
        raised = raised + jnp.exp(tile - peak)
        added = added + tile
    return jnp.where(iota(peak.shape, 0) == 0, peak + jnp.log(raised), added)


def program_body(
    q_hbm, k_hbm, v_hbm, node_hbm, par_hbm, pos_hbm, ow_hbm, resid_hbm, gain_ref,
    w_hbm, leaf_hbm, target_hbm, old_hbm, adv_hbm,
    token_ref, leaf_out, loss_ref,
    q_ref, k_ref, v_ref, node_ref, par_ref, pos_ref, resid_ref, leaf_ref, target_ref, old_ref, adv_ref,
    in_sems, *rest,
):
    front_count = len(front_scratch())
    front_refs = rest[:front_count]
    (
        w, part_a, part_b, part_c, logits, paths, tiny, info, info_x, info_z, info_y,
        stat_s, stat_y, stat_x, stat_z, mine, mine_x, last_s, last_r,
        w_sem, w_ss, w_rs, g_ss, g_rs, i_ss, i_rs, t_ss, t_rs, l_ss, l_rs,
    ) = rest[front_count:]
    grp = lax.axis_index("grp")
    me = lax.axis_index("seg")
    y = grp // 2
    core = lax.rem(grp, 2)
    z = me // X
    x = lax.rem(me, X)
    at = {"x": x, "y": y, "z": z}
    size = {"x": X, "y": Y, "z": Z}

    def peer(axis, delta):
        moved = dict(at)
        moved[axis] = lax.rem(at[axis] + delta + size[axis], size[axis])
        return {"grp": moved["y"] * 2 + core, "seg": moved["z"] * X + moved["x"]}

    barrier = pltpu.get_barrier_semaphore()
    offsets = [way * delta for delta in range(1, WINDOW) for way in (1, -1)]
    offsets += [delta for delta in range(X, SEG, X) if min(delta, SEG - delta) >= WINDOW]
    partners = [{"seg": lax.rem(me + delta + SEG, SEG)} for delta in offsets]
    partners += [{"grp": lax.rem(grp + delta, GRP)} for delta in range(1, GRP)]
    for partner in partners:
        pl.semaphore_signal(barrier, 1, device_id=partner)
    loads = []
    for index, (src, dst) in enumerate(
        (
            (q_hbm, q_ref), (k_hbm, k_ref), (v_hbm, v_ref), (node_hbm, node_ref), (par_hbm, par_ref),
            (pos_hbm, pos_ref), (resid_hbm, resid_ref), (leaf_hbm, leaf_ref),
            (target_hbm, target_ref), (old_hbm, old_ref), (adv_hbm, adv_ref),
        )
    ):
        copy = pltpu.make_async_copy(src, dst, in_sems.at[index])
        copy.start()
        loads.append(copy)
    own_w = pltpu.make_async_copy(w_hbm, w.at[:, 0:VOC], w_sem)
    loads[0].wait()

    tile_sub = iota((8, ROWS), 0)
    tile_lane = iota((8, ROWS), 1)
    pending = []
    swap = pltpu.make_async_remote_copy(
        src_ref=w_hbm,
        dst_ref=w.at[:, VOC : 2 * VOC],
        send_sem=w_ss,
        recv_sem=w_rs,
        device_id={"grp": y * 2 + 1 - core, "seg": me},
    )

    def spread(axis, sources, into, base, ss, rs):
        count = size[axis]
        here = at[axis]
        for delta in range(1, count):
            there = lax.rem(here + delta, count)
            copy = pltpu.make_async_remote_copy(
                src_ref=sources(there),
                dst_ref=into.at[here],
                send_sem=ss.at[base + delta],
                recv_sem=rs.at[base + here],
                device_id=peer(axis, delta),
            )
            copy.start()
            pending.append(copy)

    def collect(axis, into, base, ss, rs):
        count = size[axis]
        here = at[axis]
        for delta in range(1, count):
            there = lax.rem(here + delta, count)
            pltpu.make_async_remote_copy(
                src_ref=into.at[there],
                dst_ref=into.at[there],
                send_sem=ss.at[base + delta],
                recv_sem=rs.at[base + there],
                device_id=peer(axis, delta),
            ).wait_recv()

    def gather(part, buf, order):
        ready = []
        for stage, axis in enumerate(order):
            count = size[axis]
            done = order[:stage]

            def block(index, half):
                where = []
                for name in "xyz":
                    if name == axis:
                        where.append(lax.rem(index + 2 * count, count))
                    elif name not in done:
                        where.append(at[name])
                    elif half is not None and name == done[0]:
                        cut = size[name] // 2
                        where.append(pl.ds(half * cut, cut))
                    else:
                        where.append(slice(None))
                return buf.at[tuple(where)]

            def ring(step, way):
                half = None
                if step == count // 2:
                    if stage == 0:
                        if way < 0:
                            return None
                    else:
                        half = 0 if way > 0 else 1
                index = ((part * 3 + stage) * 4 + step - 1) * 2 + (way < 0)
                sent = block(at[axis] - way * (step - 1), half)
                landed = block(at[axis] - way * step, half)
                send = pltpu.make_async_remote_copy(
                    src_ref=sent,
                    dst_ref=sent,
                    send_sem=g_ss.at[index],
                    recv_sem=g_rs.at[index],
                    device_id=peer(axis, way),
                )
                arrive = pltpu.make_async_remote_copy(
                    src_ref=landed,
                    dst_ref=landed,
                    send_sem=g_ss.at[index],
                    recv_sem=g_rs.at[index],
                    device_id=peer(axis, way),
                )
                return send, arrive

            for step in range(1, count // 2 + 1):
                for copy in ready:
                    copy.wait_recv()
                ready = []
                for way in (1, -1):
                    both = ring(step, way)
                    if both is not None:
                        both[0].start()
                        pending.append(both[0])
                        ready.append(both[1])
                yield
        for copy in ready:
            copy.wait_recv()

    def tell():
        tiny[...] = jnp.zeros_like(tiny)
        tiny[0:1, 0:SCORE] = target_ref[...].astype(F32)
        tiny[1:2, 0:SCORE] = old_ref[...]
        tiny[2:3, 0:2] = adv_ref[...]
        start = tiny[...]
        info[...] = jnp.where(
            tile_sub < 2, pltpu.roll(start, SCORE * me, 1), pltpu.roll(start, 2 * me, 1)
        )
        info_x[x] = info[...]
        spread("x", lambda there: info_x.at[x], info_x, 0, i_ss, i_rs)
        yield
        collect("x", info_x, 0, i_ss, i_rs)
        info_z[z] = info_x[0] + info_x[1] + info_x[2] + info_x[3]
        spread("z", lambda there: info_z.at[z], info_z, X, i_ss, i_rs)
        yield
        collect("z", info_z, X, i_ss, i_rs)
        whole = info_z[0]
        for index in range(1, Z):
            whole = whole + info_z[index]
        info_y[y] = whole
        spread("y", lambda there: info_y.at[y], info_y, X + Z, i_ss, i_rs)
        yield
        collect("y", info_y, X + Z, i_ss, i_rs)

    talk = tell()

    def greet():
        pl.semaphore_wait(barrier, len(partners))

    def early():
        own_w.start()
        swap.start()
        for copy in loads[1:]:
            copy.wait()
        next(talk)

    def middle(closure_t, row_hot_t):
        next(talk)
        leaf_hot_t = hot(iota((NODES, LEAVES), 0) == leaf_ref[...])
        leaf_reach_t = mm(closure_t, leaf_hot_t)
        filler = jnp.zeros((NODES, NODES - LEAVES), F32)
        leaf_reach = jnp.concatenate([leaf_reach_t, filler], axis=1).T
        paths[...] = mm(leaf_reach.astype(BF16), row_hot_t)

    normed, drain = front(
        me, grp, q_ref, k_ref, v_ref, node_ref, par_ref, pos_ref, ow_hbm, resid_ref, gain_ref,
        *front_refs, greet, early, middle,
    )
    bufs = (part_a, part_b, part_c)
    for (offset, width, order), buf in zip(PARTS, bufs):
        buf[x, y, z] = normed[:, offset : offset + width]
    next(talk)
    running = [
        gather(part, buf, order) for part, ((offset, width, order), buf) in enumerate(zip(PARTS, bufs))
    ]
    while running:
        for item in list(running):
            try:
                next(item)
            except StopIteration:
                running.remove(item)
    for rest_of in talk:
        pass

    own_w.wait()
    swap.wait_recv()

    def columns(n, carry):
        cols = pl.ds(pl.multiple_of(256 * n, 256), 256)
        total = None
        for (offset, width, order), buf in zip(PARTS, bufs):
            for index in range(X):
                rows = buf[index].reshape(Y * Z * 16, width)
                term = mm(rows, w[DX * index + offset : DX * index + offset + width, cols])
                total = term if total is None else total + term
        logits[:, cols] = total
        return carry

    lax.fori_loop(0, 2 * VOC // 256, columns, 0)

    voc_lane = iota((ROWS, 2 * VOC), 1)
    own_base = (grp * SEG + me) * VOC
    other_base = ((2 * y + 1 - core) * SEG + me) * VOC - VOC
    voc_id = (voc_lane + jnp.where(voc_lane < VOC, own_base, other_base)).astype(F32)
    targets = jnp.concatenate(
        [info_y[...].reshape(8 * Y, ROWS), jnp.zeros((ROWS - 8 * Y, ROWS), F32)], axis=0
    ).T
    square_lane = iota((ROWS, ROWS), 1)
    for index in range(Y):
        block = logits[ROWS * index : ROWS * index + ROWS, :]
        top = jnp.max(block, axis=1, keepdims=True)
        lse = top + jnp.log(jnp.sum(jnp.exp(block - top), axis=1, keepdims=True))
        found = voc_id == targets[:, 8 * index : 8 * index + 1]
        picked = jnp.sum(jnp.where(found, block, 0.0), axis=1, keepdims=True)
        both = jnp.where(square_lane == 0, lse, jnp.where(square_lane == 1, picked, 0.0))
        stat_s[index] = both.T[0:8]
    spread("y", lambda there: stat_s.at[there], stat_y, 0, t_ss, t_rs)
    stat_y[y] = stat_s[y]

    path = paths[...]
    counts = jnp.maximum(jnp.sum(path, axis=1, keepdims=True), 1.0)
    collect("y", stat_y, 0, t_ss, t_rs)
    mine[...] = merge_tiles([stat_y[index] for index in range(Y)])
    spread("x", lambda there: mine, stat_x, Y, t_ss, t_rs)
    stat_x[x] = mine[...]
    collect("x", stat_x, Y, t_ss, t_rs)
    mine_x[...] = merge_tiles([stat_x[index] for index in range(X)])
    spread("z", lambda there: mine_x, stat_z, Y + X, t_ss, t_rs)
    stat_z[z] = mine_x[...]
    collect("z", stat_z, Y + X, t_ss, t_rs)
    merged = merge_tiles([stat_z[index] for index in range(Z)])

    own_info = info_y[y]
    token_row = merged[1:2] - merged[0:1] - own_info[1:2]
    shift = lax.rem(ROWS - SCORE * me, ROWS)
    token_ref[...] = pltpu.roll(jnp.broadcast_to(token_row, (8, ROWS)), shift, 1)[0:1, 0:SCORE]
    means = jnp.sum(path * token_row, axis=1, keepdims=True) / counts
    leaf_row = jnp.broadcast_to(means, (ROWS, ROWS)).T[0:8]
    leaf_out[...] = pltpu.roll(leaf_row, lax.rem(ROWS - 2 * me, ROWS), 1)[0:1, 0:2]
    gains = own_info[2:3]
    ratio = jnp.exp(leaf_row)
    terms = jnp.minimum(ratio * gains, jnp.clip(ratio, 1.0 - EPS_LOW, 1.0 + EPS_HIGH) * gains)
    terms = jnp.where((tile_sub == 0) & (tile_lane < LEAVES), terms, 0.0)
    last_s[...] = terms

    last = []
    for delta in range(1, GRP):
        copy = pltpu.make_async_remote_copy(
            src_ref=last_s,
            dst_ref=last_r.at[grp],
            send_sem=l_ss.at[delta],
            recv_sem=l_rs.at[grp],
            device_id={"grp": lax.rem(grp + delta, GRP), "seg": me},
        )
        copy.start()
        last.append(copy)
    last_r[grp] = terms
    for delta in range(1, GRP):
        there = lax.rem(grp + delta, GRP)
        pltpu.make_async_remote_copy(
            src_ref=last_s,
            dst_ref=last_r.at[there],
            send_sem=l_ss.at[delta],
            recv_sem=l_rs.at[there],
            device_id={"grp": there, "seg": me},
        ).wait_recv()
    everything = last_r[0]
    for index in range(1, GRP):
        everything = everything + last_r[index]
    loss_ref[...] = -jnp.sum(everything, axis=(0, 1), keepdims=True) / (LEAVES * GRP)

    drain()
    for copy in pending:
        copy.wait_send()
    swap.wait_send()
    for copy in last:
        copy.wait_send()


def body(
    queries, keys, values, node_ids, parents, score_pos, out_weight, resid, norm_gain,
    vocab_weight, targets, old_logp, leaf_node, advantages,
):
    sems = pltpu.SemaphoreType.DMA
    tile = pltpu.VMEM((8, ROWS), F32)

    def tiles(count):
        return pltpu.VMEM((count, 8, ROWS), F32)

    anywhere = pl.BlockSpec(memory_space=pl.ANY)
    token, leaf, loss = pl.pallas_call(
        program_body,
        out_shape=(
            jax.ShapeDtypeStruct((1, SCORE), F32),
            jax.ShapeDtypeStruct((1, 2), F32),
            jax.ShapeDtypeStruct((1, 1), F32),
        ),
        in_specs=[anywhere] * 8 + [vmem()] + [anywhere] * 5,
        out_specs=(vmem(), vmem(), vmem()),
        scratch_shapes=[
            pltpu.VMEM((SCORE, 64 * HEAD), BF16),
            pltpu.VMEM((TOK, KV_HEADS * HEAD), BF16),
            pltpu.VMEM((TOK, KV_HEADS * HEAD), BF16),
            pltpu.VMEM((SEG, TOK), jnp.int32),
            pltpu.VMEM((1, NODES), jnp.int32),
            pltpu.VMEM((1, ROWS), jnp.int32),
            pltpu.VMEM((SCORE, D), BF16),
            pltpu.VMEM((1, LEAVES), jnp.int32),
            pltpu.VMEM((1, SCORE), jnp.int32),
            pltpu.VMEM((1, SCORE), F32),
            pltpu.VMEM((1, 2), F32),
            sems((11,)),
        ]
        + front_scratch()
        + [pltpu.VMEM((D, 2 * VOC), BF16)]
        + [pltpu.VMEM((X, Y, Z, 16, width), BF16) for offset, width, order in PARTS]
        + [
            pltpu.VMEM((Y * ROWS, 2 * VOC), F32),
            pltpu.VMEM((NODES, ROWS), F32),
            tile,
            tile,
            tiles(X),
            tiles(Z),
            tiles(Y),
            tiles(Y),
            tiles(Y),
            tiles(X),
            tiles(Z),
            tile,
            tile,
            tile,
            tiles(GRP),
            sems,
            sems,
            sems,
            sems((72,)),
            sems((72,)),
            sems((X + Y + Z,)),
            sems((X + Y + Z,)),
            sems((X + Y + Z,)),
            sems((X + Y + Z,)),
            sems((GRP,)),
            sems((GRP,)),
        ],
        compiler_params=pltpu.CompilerParams(
            collective_id=0, has_side_effects=True, vmem_limit_bytes=58 * MIB
        ),
    )(
        queries[0], keys[0], values[0], node_ids.reshape(SEG, TOK), parents, score_pos, out_weight,
        resid[0], norm_gain.reshape(1, D), vocab_weight, leaf_node, targets, old_logp, advantages,
    )
    return (token, leaf, loss.reshape(()))


def solution(mesh):
    placed = (
        P("grp", "seg", None),
        P("grp", "seg", None),
        P("grp", "seg", None),
        P("grp", None),
        P("grp", None),
        P("grp", None),
        P("seg", None),
        P("grp", "seg", None),
        P(),
        P(None, ("grp", "seg")),
        P("grp", "seg"),
        P("grp", "seg"),
        P("grp", None),
        P("grp", "seg"),
    )
    return jax.shard_map(
        body,
        mesh=mesh,
        in_specs=placed,
        out_specs=(P("grp", "seg"), P("grp", "seg"), P()),
        check_vma=False,
    )
```

time: 168 us -> 142 us (0.85)
  Pallas kernels: 154 us -> 136 us
  local copies, waits for them, and re-layouts: 10.8 us -> 3.64 us
    pallas_call x2 -> x1, Pallas kernels: 154 us -> 136 us  [body(): pl.pallas_call(program_body, out_shape=(jax.ShapeDtypeStruct((1, SCORE),...]
    unnamed x20 -> x2, local copies, waits for them, and re-layouts: 10.1 us -> 2.32 us
where the time goes in v1:
time: 142 us
  Pallas kernels  136 us (96%)
  local copies, waits for them, and re-layouts  3.64 us (3%)
  between operations  2.39 us (2%)
    pallas_call x1, Pallas kernels, body(): pl.pallas_call(program_body, out_shape=(jax.ShapeDtypeStruct((1, SCORE),...  136 us

profile of v1, /device:TPU:1, one launch (start us, length us, event | category | flops | bytes accessed | tf_op | source)
XLA Modules:
  0.0 141.9 jit_solution(15049027625148453494)
XLA Ops:
  0.6 1.3 reshape.16.gain_ref
  1.9 135.8 %shard_map.157 = (f32[1,4]{1,0:T(1,128)}, f32[1,2]{1,0:T(1,128)}, f32[1,1]{1,0:T(1,128)}) custom-call(bf16[4,8192]{1,0:T(4,128)(2,1)} %bitcast.8, bf16[128,1024]{1,0:T(8,128)(2,1)} %bitcast.6, bf16[128,1024]{1,0:T(8,128)(2,1)} %bitcast.7, s32[32,128]{1,0:T(8,128)} %bitcast.10, s32[1,128]{1,0:T(1,128)} %par_hbm.1, s32[1,128]{1,0:T(1,128)} %pos_hbm.1, ...), custom_call_target="tpu_custom_call" | custom-call | tf_op jit(solution)/shard_map/pallas_call | solution.py:752
  137.8 1.2 copy.20
  139.0 1.1 copy.21

commit v2 on v1

--- a/solution.py
+++ b/solution.py
@@ -26,7 +26,7 @@
 D = 5120
 DX = D // X
 VOC = 384
-PARTS = ((0, 512, "xyz"), (512, 384, "yzx"), (896, 384, "zxy"))
+PARTS = ((0, 384, "yxz"), (384, 512, "yzx"), (896, 384, "zxy"))
 MIB = 1024 * 1024
 
 
@@ -125,26 +125,7 @@
                 {"seg": lax.rem(me - slot + SEG, SEG)},
             )
 
-    slab = pl.ds(pl.multiple_of(32 * grp, 32), 32)
-    for delta in range(1, X):
-        send(
-            ow_hbm.at[slab, dx_cols(lax.rem(x + delta, X))],
-            wx.at[delta - 1, slab],
-            wx_ss.at[delta - 1],
-            wx_rs.at[delta - 1],
-            at_x(delta),
-        )
     early()
-
-    place_row = iota((16, 16), 0)
-    place_col = iota((16, 16), 1)
-    place = hot((place_row == SCORE * x + place_col) & (place_col < SCORE))
-    for delta in range(X):
-        cols = resid_ref[:, dx_cols(lax.rem(x + delta, X))]
-        padded = jnp.concatenate([cols.astype(F32), jnp.zeros((16 - SCORE, DX), F32)], axis=0)
-        rsend[delta] = mm(place, padded.astype(BF16)).astype(BF16)
-        if delta:
-            send(rsend.at[delta], rrecv.at[delta - 1], r_ss.at[delta], r_rs.at[delta], at_x(delta))
 
     closure_t = closure_transposed(par_ref[...])
     position_row = pos_ref[...]
@@ -192,17 +173,21 @@
                     {"seg": lax.rem(me + way + SEG, SEG)},
                 )
 
+    core = lax.rem(grp, 2)
+    level = grp // 2
+
+    def slab_of(plane, height):
+        return pl.ds(pl.multiple_of(32 * (Y * plane + height), 32), 32)
+
+    slab = slab_of(core, level)
     for delta in range(1, X):
-        landed(wx.at[delta - 1, slab], wx_ss.at[delta - 1], wx_rs.at[delta - 1], at_x(delta))
-    for delta in range(1, GRP):
         send(
-            wx.at[:, slab],
-            wx.at[:, slab],
-            wy_ss.at[delta],
-            wy_rs.at[grp],
-            {"grp": lax.rem(grp + delta, GRP), "seg": me},
+            ow_hbm.at[slab, dx_cols(lax.rem(x + delta, X))],
+            wx.at[delta - 1, slab],
+            wx_ss.at[delta - 1],
+            wx_rs.at[delta - 1],
+            at_x(delta),
         )
-
     part_slot = iota((4, 2 * ROWS), 1) // 32
     for c in range(2):
         tops = []
@@ -247,6 +232,26 @@
                     at_x(delta),
                 )
 
+    for delta in range(1, X):
+        landed(wx.at[delta - 1, slab], wx_ss.at[delta - 1], wx_rs.at[delta - 1], at_x(delta))
+    for delta in range(1, Y):
+        send(
+            wx.at[:, slab],
+            wx.at[:, slab],
+            wy_ss.at[delta],
+            wy_rs.at[level],
+            {"grp": 2 * lax.rem(level + delta, Y) + core, "seg": me},
+        )
+    place_row = iota((16, 16), 0)
+    place_col = iota((16, 16), 1)
+    place = hot((place_row == SCORE * x + place_col) & (place_col < SCORE))
+    for delta in range(X):
+        cols = resid_ref[:, dx_cols(lax.rem(x + delta, X))]
+        padded = jnp.concatenate([cols.astype(F32), jnp.zeros((16 - SCORE, DX), F32)], axis=0)
+        rsend[delta] = mm(place, padded.astype(BF16)).astype(BF16)
+        if delta:
+            send(rsend.at[delta], rrecv.at[delta - 1], r_ss.at[delta], r_rs.at[delta], at_x(delta))
+
     guarded = []
     for c in range(2):
         for step in range(4):
@@ -288,6 +293,21 @@
                 pending.append(away_copy)
 
     middle(closure_t, row_hot_t)
+    for delta in range(1, Y):
+        other = lax.rem(level + delta, Y)
+        landed(
+            wx.at[:, slab_of(core, other)],
+            wy_ss.at[delta],
+            wy_rs.at[other],
+            {"grp": 2 * other + core, "seg": me},
+        )
+    send(
+        wx.at[:, pl.ds(pl.multiple_of(ROWS * core, ROWS), ROWS)],
+        wx.at[:, pl.ds(pl.multiple_of(ROWS * core, ROWS), ROWS)],
+        wy_ss.at[Y],
+        wy_rs.at[Y],
+        {"grp": 2 * level + 1 - core, "seg": me},
+    )
 
     for delta in range(1, Z):
         source = lax.rem(z + delta, Z)
@@ -312,10 +332,12 @@
         send(mixs, mixr.at[delta - 1], m_ss.at[delta - 1], m_rs.at[delta - 1], at_x(delta))
     own_weight.wait()
     product = mm(left, wown[...])
-    for delta in range(1, GRP):
-        other = lax.rem(grp + delta, GRP)
-        theirs = pl.ds(pl.multiple_of(32 * other, 32), 32)
-        landed(wx.at[:, theirs], wy_ss.at[delta], wy_rs.at[other], {"grp": other, "seg": me})
+    landed(
+        wx.at[:, pl.ds(pl.multiple_of(ROWS * (1 - core), ROWS), ROWS)],
+        wy_ss.at[Y],
+        wy_rs.at[Y],
+        {"grp": 2 * level + 1 - core, "seg": me},
+    )
     for delta in (1, 3, 2):
         landed(mixr.at[delta - 1], m_ss.at[delta - 1], m_rs.at[delta - 1], at_x(delta))
         product = product + mm(mixr[delta - 1], wx[delta - 1])
@@ -336,7 +358,7 @@
     sqs[...] = jnp.broadcast_to(squares, sqs.shape)
     for delta in (1, 3, 2):
         send(sqs, sqr.at[delta - 1], s_ss.at[delta - 1], s_rs.at[delta - 1], at_x(delta))
-    gain = gain_ref[:, dx_cols(x)].astype(F32)
+    gain = gain_ref[dx_cols(x)].astype(F32).reshape(1, DX)
     for delta in (1, 3, 2):
         landed(sqr.at[delta - 1], s_ss.at[delta - 1], s_rs.at[delta - 1], at_x(delta))
     power = (sqs[...] + sqr[0] + sqr[1] + sqr[2])[:, 0:1] / D
@@ -417,6 +439,119 @@
     return pl.BlockSpec(memory_space=pltpu.VMEM)
 
 
+SIZE = {"x": X, "y": Y, "z": Z}
+
+
+def plan_gather():
+    messages = []
+    by_key = {}
+    for part, (offset, width, order) in enumerate(PARTS):
+        for stage, axis in enumerate(order):
+            count = SIZE[axis]
+            chunked = stage == 2
+            inner = range(SIZE[order[1]]) if chunked else (None,)
+            amount = 32 * width
+            for name in order[:stage]:
+                amount *= SIZE[name]
+            if chunked:
+                amount //= SIZE[order[1]]
+            for step in range(1, count // 2 + 1):
+                for rank, chunk in enumerate(inner):
+                    for way in (1, -1):
+                        half = None
+                        if step == count // 2:
+                            if chunked:
+                                if (way > 0) != (rank % 2 == 0):
+                                    continue
+                            elif stage == 0:
+                                if way < 0:
+                                    continue
+                            else:
+                                half = 0 if way > 0 else 1
+                        key = (part, stage, step, chunk, way)
+                        by_key[key] = len(messages)
+                        messages.append(
+                            dict(
+                                part=part, stage=stage, axis=axis, step=step, chunk=chunk, way=way, half=half,
+                                size=amount if half is None else amount // 2,
+                            )
+                        )
+
+    def bringing(part, stage, offset):
+        count = SIZE[PARTS[part][2][stage]]
+        offset %= count
+        if offset == 0:
+            return []
+        found = []
+        for key, index in by_key.items():
+            if key[0] == part and key[1] == stage and (-key[4] * key[2]) % count == offset:
+                found.append(index)
+        return found
+
+    def whole_stage(part, stage):
+        return [index for key, index in by_key.items() if key[0] == part and key[1] == stage]
+
+    for message in messages:
+        part, stage = message["part"], message["stage"]
+        if message["step"] > 1:
+            if message["chunk"] is None:
+                needs = bringing(part, stage, -message["way"] * (message["step"] - 1))
+            else:
+                needs = [by_key[part, stage, message["step"] - 1, message["chunk"], message["way"]]]
+        elif stage == 0:
+            needs = []
+        elif stage == 1:
+            needs = whole_stage(part, 0)
+        elif message["chunk"] == 0:
+            needs = whole_stage(part, 0)
+        else:
+            needs = bringing(part, 1, message["chunk"])
+        message["needs"] = needs
+    tasks = []
+    for part, (offset, width, order) in enumerate(PARTS):
+        count = SIZE[order[2]]
+        groups = [(0,)] + [(step, -step) for step in range(1, count // 2)] + [(count // 2,)]
+        if part == 1:
+            groups = [(item,) for group in groups for item in group]
+        for group in groups:
+            needs = []
+            for item in group:
+                if item == 0:
+                    needs += whole_stage(part, 0) + whole_stage(part, 1)
+                else:
+                    needs += bringing(part, 2, item)
+            tasks.append(dict(part=part, group=group, needs=needs))
+
+    free = {}
+    ready = {}
+    arrive = {}
+    left = set(range(len(messages)))
+    while left:
+        best = None
+        for index in sorted(left):
+            message = messages[index]
+            if all(need in arrive for need in message["needs"]):
+                at = max([arrive[need] for need in message["needs"]], default=0.0)
+                link = (message["axis"], message["way"])
+                begin = max(at, free.get(link, 0.0))
+                if best is None or (begin, at, index) < best[0]:
+                    best = ((begin, at, index), index, link, at)
+        (begin, at, unused), index, link, at = best
+        left.remove(index)
+        finish = begin + messages[index]["size"] / 46e3
+        free[link] = finish
+        ready[index] = at
+        arrive[index] = finish + 0.9
+    events = [(ready[index], 0, index) for index in ready]
+    events += [
+        (max(arrive[need] for need in task["needs"]) + 0.2, 1, number) for number, task in enumerate(tasks)
+    ]
+    return messages, tasks, sorted(events)
+
+
+GATHERS = len(plan_gather()[0])
+
+
 def merge_tiles(tiles):
     peak = tiles[0]
     for tile in tiles[1:]:
@@ -432,7 +567,7 @@
 def program_body(
     q_hbm, k_hbm, v_hbm, node_hbm, par_hbm, pos_hbm, ow_hbm, resid_hbm, gain_ref,
     w_hbm, leaf_hbm, target_hbm, old_hbm, adv_hbm,
-    token_ref, leaf_out, loss_ref,
+    answer_ref,
     q_ref, k_ref, v_ref, node_ref, par_ref, pos_ref, resid_ref, leaf_ref, target_ref, old_ref, adv_ref,
     in_sems, *rest,
 ):
@@ -440,8 +575,8 @@
     front_refs = rest[:front_count]
     (
         w, part_a, part_b, part_c, logits, paths, tiny, info, info_x, info_z, info_y,
-        stat_s, stat_y, stat_x, stat_z, mine, mine_x, last_s, last_r,
-        w_sem, w_ss, w_rs, g_ss, g_rs, i_ss, i_rs, t_ss, t_rs, l_ss, l_rs,
+        stat_s, stat_y, stat_z, mine_x, last_s, last_r,
+        w_sem, w_ss, w_rs, g_ss, g_rs, i_ss, i_rs, t_ss, t_rs, y_ss, y_rs, l_ss, l_rs,
     ) = rest[front_count:]
     grp = lax.axis_index("grp")
     me = lax.axis_index("seg")
@@ -461,7 +596,12 @@
     offsets = [way * delta for delta in range(1, WINDOW) for way in (1, -1)]
     offsets += [delta for delta in range(X, SEG, X) if min(delta, SEG - delta) >= WINDOW]
     partners = [{"seg": lax.rem(me + delta + SEG, SEG)} for delta in offsets]
-    partners += [{"grp": lax.rem(grp + delta, GRP)} for delta in range(1, GRP)]
+    partners += [{"grp": lax.rem(grp + delta, GRP), "seg": me} for delta in range(1, GRP)]
+    partners += [
+        {"grp": lax.rem(y + dy, Y) * 2 + core, "seg": z * X + lax.rem(x + dx, X)}
+        for dy in range(1, Y)
+        for dx in range(1, X)
+    ]
     for partner in partners:
         pl.semaphore_signal(barrier, 1, device_id=partner)
     loads = []
@@ -517,66 +657,72 @@
                 device_id=peer(axis, delta),
             ).wait_recv()
 
-    def gather(part, buf, order):
-        ready = []
-        for stage, axis in enumerate(order):
-            count = size[axis]
-            done = order[:stage]
-
-            def block(index, half):
-                where = []
-                for name in "xyz":
-                    if name == axis:
-                        where.append(lax.rem(index + 2 * count, count))
-                    elif name not in done:
-                        where.append(at[name])
-                    elif half is not None and name == done[0]:
-                        cut = size[name] // 2
-                        where.append(pl.ds(half * cut, cut))
-                    else:
-                        where.append(slice(None))
-                return buf.at[tuple(where)]
-
-            def ring(step, way):
-                half = None
-                if step == count // 2:
-                    if stage == 0:
-                        if way < 0:
-                            return None
-                    else:
-                        half = 0 if way > 0 else 1
-                index = ((part * 3 + stage) * 4 + step - 1) * 2 + (way < 0)
-                sent = block(at[axis] - way * (step - 1), half)
-                landed = block(at[axis] - way * step, half)
-                send = pltpu.make_async_remote_copy(
-                    src_ref=sent,
-                    dst_ref=sent,
-                    send_sem=g_ss.at[index],
-                    recv_sem=g_rs.at[index],
-                    device_id=peer(axis, way),
-                )
-                arrive = pltpu.make_async_remote_copy(
-                    src_ref=landed,
-                    dst_ref=landed,
-                    send_sem=g_ss.at[index],
-                    recv_sem=g_rs.at[index],
-                    device_id=peer(axis, way),
-                )
-                return send, arrive
-
-            for step in range(1, count // 2 + 1):
-                for copy in ready:
-                    copy.wait_recv()
-                ready = []
-                for way in (1, -1):
-                    both = ring(step, way)
-                    if both is not None:
-                        both[0].start()
-                        pending.append(both[0])
-                        ready.append(both[1])
-                yield
-        for copy in ready:
-            copy.wait_recv()
+    bufs = (part_a, part_b, part_c)
+    messages, tasks, events = plan_gather()
+
+    def block(message, moved):
+        axis, stage = message["axis"], message["stage"]
+        order = PARTS[message["part"]][2]
+        where = []
+        for name in "xyz":
+            if name == axis:
+                where.append(lax.rem(at[name] + moved + 2 * size[name], size[name]))
+            elif name not in order[:stage]:
+                where.append(at[name])
+            elif message["chunk"] is not None and name == order[1]:
+                where.append(lax.rem(at[name] + message["chunk"], size[name]))
+            elif message["half"] is not None and name == order[0]:
+                cut = size[name] // 2
+                where.append(pl.ds(message["half"] * cut, cut))
+            else:
+                where.append(slice(None))
+        return bufs[message["part"]].at[tuple(where)]
+
+    def ring(index, moved):
+        message = messages[index]
+        ref = block(message, moved)
+        return pltpu.make_async_remote_copy(
+            src_ref=ref,
+            dst_ref=ref,
+            send_sem=g_ss.at[index],
+            recv_sem=g_rs.at[index],
+            device_id=peer(message["axis"], message["way"]),
+        )
+
+    def head_task(task):
+        part = task["part"]
+        offset, width, order = PARTS[part]
+        buf = bufs[part]
+        axis = order[2]
+
+        def columns(n, carry):
+            cols = pl.ds(pl.multiple_of(256 * n, 256), 256)
+            if axis == "x":
+                here = lax.rem(x + task["group"][0] + X, X)
+                rows = buf[here].reshape(Y * Z * 16, width)
+                weight = w[pl.ds(pl.multiple_of(DX * here + offset, 128), width), cols]
+                logits[:, :, :, cols] = logits[:, :, :, cols] + mm(rows, weight).reshape(Y, Z, 16, 256)
+                return carry
+            places = [lax.rem(at[axis] + item + size[axis], size[axis]) for item in task["group"]]
+            total = None
+            for index in range(X):
+                if axis == "z":
+                    rows = [buf[index, :, place].reshape(Y * 16, width) for place in places]
+                else:
+                    rows = [buf[index, place].reshape(Z * 16, width) for place in places]
+                rows = rows[0] if len(rows) == 1 else jnp.concatenate(rows, axis=0)
+                term = mm(rows, w[DX * index + offset : DX * index + offset + width, cols])
+                total = term if total is None else total + term
+            high = total.shape[0] // len(places)
+            for number, place in enumerate(places):
+                piece = total[high * number : high * number + high]
+                if axis == "z":
+                    logits[:, place, :, cols] = logits[:, place, :, cols] + piece.reshape(Y, 16, 256)
+                else:
+                    logits[place, :, :, cols] = logits[place, :, :, cols] + piece.reshape(Z, 16, 256)
+            return carry
+
+        lax.fori_loop(0, 2 * VOC // 256, columns, 0)
 
     def tell():
         tiny[...] = jnp.zeros_like(tiny)
@@ -617,6 +763,7 @@
 
     def middle(closure_t, row_hot_t):
         next(talk)
+        logits[...] = jnp.zeros_like(logits)
         leaf_hot_t = hot(iota((NODES, LEAVES), 0) == leaf_ref[...])
         leaf_reach_t = mm(closure_t, leaf_hot_t)
         filler = jnp.zeros((NODES, NODES - LEAVES), F32)
@@ -627,37 +774,33 @@
         me, grp, q_ref, k_ref, v_ref, node_ref, par_ref, pos_ref, ow_hbm, resid_ref, gain_ref,
         *front_refs, greet, early, middle,
     )
-    bufs = (part_a, part_b, part_c)
     for (offset, width, order), buf in zip(PARTS, bufs):
         buf[x, y, z] = normed[:, offset : offset + width]
     next(talk)
-    running = [
-        gather(part, buf, order) for part, ((offset, width, order), buf) in enumerate(zip(PARTS, bufs))
-    ]
-    while running:
-        for item in list(running):
-            try:
-                next(item)
-            except StopIteration:
-                running.remove(item)
+    seen = set()
+
+    def await_all(needs):
+        for index in needs:
+            if index not in seen:
+                seen.add(index)
+                ring(index, -messages[index]["way"] * messages[index]["step"]).wait_recv()
+
+    loaded = False
+    for unused, kind, index in events:
+        if kind == 0:
+            await_all(messages[index]["needs"])
+            copy = ring(index, -messages[index]["way"] * (messages[index]["step"] - 1))
+            copy.start()
+            pending.append(copy)
+        else:
+            if not loaded:
+                own_w.wait()
+                swap.wait_recv()
+                loaded = True
+            await_all(tasks[index]["needs"])
+            head_task(tasks[index])
     for rest_of in talk:
         pass
-
-    own_w.wait()
-    swap.wait_recv()
-
-    def columns(n, carry):
-        cols = pl.ds(pl.multiple_of(256 * n, 256), 256)
-        total = None
-        for (offset, width, order), buf in zip(PARTS, bufs):
-            for index in range(X):
-                rows = buf[index].reshape(Y * Z * 16, width)
-                term = mm(rows, w[DX * index + offset : DX * index + offset + width, cols])
-                total = term if total is None else total + term
-        logits[:, cols] = total
-        return carry
-
-    lax.fori_loop(0, 2 * VOC // 256, columns, 0)
 
     voc_lane = iota((ROWS, 2 * VOC), 1)
     own_base = (grp * SEG + me) * VOC
@@ -668,24 +811,45 @@
     ).T
     square_lane = iota((ROWS, ROWS), 1)
     for index in range(Y):
-        block = logits[ROWS * index : ROWS * index + ROWS, :]
+        block = logits[index].reshape(ROWS, 2 * VOC)
         top = jnp.max(block, axis=1, keepdims=True)
         lse = top + jnp.log(jnp.sum(jnp.exp(block - top), axis=1, keepdims=True))
         found = voc_id == targets[:, 8 * index : 8 * index + 1]
         picked = jnp.sum(jnp.where(found, block, 0.0), axis=1, keepdims=True)
         both = jnp.where(square_lane == 0, lse, jnp.where(square_lane == 1, picked, 0.0))
         stat_s[index] = both.T[0:8]
-    spread("y", lambda there: stat_s.at[there], stat_y, 0, t_ss, t_rs)
-    stat_y[y] = stat_s[y]
+    def square(dy, dx):
+        ty = lax.rem(y + dy, Y)
+        tx = lax.rem(x + dx, X)
+        device = {"grp": ty * 2 + core, "seg": z * X + tx}
+        return ty, tx, device
+
+    steps = [(dy, dx) for dy in range(Y) for dx in range(X) if dy or dx]
+    for dy, dx in steps:
+        ty, tx, device = square(dy, dx)
+        copy = pltpu.make_async_remote_copy(
+            src_ref=stat_s.at[ty],
+            dst_ref=stat_y.at[y * X + x],
+            send_sem=y_ss.at[dy * X + dx],
+            recv_sem=y_rs.at[y * X + x],
+            device_id=device,
+        )
+        copy.start()
+        pending.append(copy)
+    stat_y[y * X + x] = stat_s[y]
 
     path = paths[...]
     counts = jnp.maximum(jnp.sum(path, axis=1, keepdims=True), 1.0)
-    collect("y", stat_y, 0, t_ss, t_rs)
-    mine[...] = merge_tiles([stat_y[index] for index in range(Y)])
-    spread("x", lambda there: mine, stat_x, Y, t_ss, t_rs)
-    stat_x[x] = mine[...]
-    collect("x", stat_x, Y, t_ss, t_rs)
-    mine_x[...] = merge_tiles([stat_x[index] for index in range(X)])
+    for dy, dx in steps:
+        ty, tx, device = square(dy, dx)
+        pltpu.make_async_remote_copy(
+            src_ref=stat_s.at[ty],
+            dst_ref=stat_y.at[ty * X + tx],
+            send_sem=y_ss.at[dy * X + dx],
+            recv_sem=y_rs.at[ty * X + tx],
+            device_id=device,
+        ).wait_recv()
+    mine_x[...] = merge_tiles([stat_y[index] for index in range(X * Y)])
     spread("z", lambda there: mine_x, stat_z, Y + X, t_ss, t_rs)
     stat_z[z] = mine_x[...]
     collect("z", stat_z, Y + X, t_ss, t_rs)
@@ -694,10 +858,10 @@
     own_info = info_y[y]
     token_row = merged[1:2] - merged[0:1] - own_info[1:2]
     shift = lax.rem(ROWS - SCORE * me, ROWS)
-    token_ref[...] = pltpu.roll(jnp.broadcast_to(token_row, (8, ROWS)), shift, 1)[0:1, 0:SCORE]
+    answer_ref[0:1, :] = pltpu.roll(jnp.broadcast_to(token_row, (8, ROWS)), shift, 1)[0:1]
     means = jnp.sum(path * token_row, axis=1, keepdims=True) / counts
     leaf_row = jnp.broadcast_to(means, (ROWS, ROWS)).T[0:8]
-    leaf_out[...] = pltpu.roll(leaf_row, lax.rem(ROWS - 2 * me, ROWS), 1)[0:1, 0:2]
+    answer_ref[1:2, :] = pltpu.roll(leaf_row, lax.rem(ROWS - 2 * me, ROWS), 1)[0:1]
     gains = own_info[2:3]
     ratio = jnp.exp(leaf_row)
     terms = jnp.minimum(ratio * gains, jnp.clip(ratio, 1.0 - EPS_LOW, 1.0 + EPS_HIGH) * gains)
@@ -728,7 +892,8 @@
     everything = last_r[0]
     for index in range(1, GRP):
         everything = everything + last_r[index]
-    loss_ref[...] = -jnp.sum(everything, axis=(0, 1), keepdims=True) / (LEAVES * GRP)
+    total = -jnp.sum(everything, axis=(0, 1), keepdims=True) / (LEAVES * GRP)
+    answer_ref[2:8, :] = jnp.broadcast_to(total, (6, ROWS))
 
     drain()
     for copy in pending:
@@ -738,6 +903,12 @@
         copy.wait_send()
 
 
+def split_body(answer_ref, token_ref, leaf_ref, loss_ref):
+    token_ref[...] = answer_ref[0:1, 0:SCORE]
+    leaf_ref[...] = answer_ref[1:2, 0:2]
+    loss_ref[...] = answer_ref[2:3, 0:1]
+
+
 def body(
     queries, keys, values, node_ids, parents, score_pos, out_weight, resid, norm_gain,
     vocab_weight, targets, old_logp, leaf_node, advantages,
@@ -749,15 +920,11 @@
         return pltpu.VMEM((count, 8, ROWS), F32)
 
     anywhere = pl.BlockSpec(memory_space=pl.ANY)
-    token, leaf, loss = pl.pallas_call(
+    answer = pl.pallas_call(
         program_body,
-        out_shape=(
-            jax.ShapeDtypeStruct((1, SCORE), F32),
-            jax.ShapeDtypeStruct((1, 2), F32),
-            jax.ShapeDtypeStruct((1, 1), F32),
-        ),
+        out_shape=jax.ShapeDtypeStruct((8, ROWS), F32),
         in_specs=[anywhere] * 8 + [vmem()] + [anywhere] * 5,
-        out_specs=(vmem(), vmem(), vmem()),
+        out_specs=vmem(),
         scratch_shapes=[
             pltpu.VMEM((SCORE, 64 * HEAD), BF16),
             pltpu.VMEM((TOK, KV_HEADS * HEAD), BF16),
@@ -776,7 +943,7 @@
         + [pltpu.VMEM((D, 2 * VOC), BF16)]
         + [pltpu.VMEM((X, Y, Z, 16, width), BF16) for offset, width, order in PARTS]
         + [
-            pltpu.VMEM((Y * ROWS, 2 * VOC), F32),
+            pltpu.VMEM((Y, Z, 16, 2 * VOC), F32),
             pltpu.VMEM((NODES, ROWS), F32),
             tile,
             tile,
@@ -784,22 +951,22 @@
             tiles(Z),
             tiles(Y),
             tiles(Y),
-            tiles(Y),
-            tiles(X),
+            tiles(X * Y),
             tiles(Z),
-            tile,
             tile,
             tile,
             tiles(GRP),
             sems,
             sems,
             sems,
-            sems((72,)),
-            sems((72,)),
+            sems((GATHERS,)),
+            sems((GATHERS,)),
             sems((X + Y + Z,)),
             sems((X + Y + Z,)),
             sems((X + Y + Z,)),
             sems((X + Y + Z,)),
+            sems((X * Y,)),
+            sems((X * Y,)),
             sems((GRP,)),
             sems((GRP,)),
         ],
@@ -808,8 +975,18 @@
         ),
     )(
         queries[0], keys[0], values[0], node_ids.reshape(SEG, TOK), parents, score_pos, out_weight,
-        resid[0], norm_gain.reshape(1, D), vocab_weight, leaf_node, targets, old_logp, advantages,
+        resid[0], norm_gain, vocab_weight, leaf_node, targets, old_logp, advantages,
     )
+    token, leaf, loss = pl.pallas_call(
+        split_body,
+        out_shape=(
+            jax.ShapeDtypeStruct((1, SCORE), F32),
+            jax.ShapeDtypeStruct((1, 2), F32),
+            jax.ShapeDtypeStruct((1, 1), F32),
+        ),
+        in_specs=[vmem()],
+        out_specs=(vmem(), vmem(), vmem()),
+    )(answer)
     return (token, leaf, loss.reshape(()))
 
 

time: 142 us -> 125 us (0.88)
  Pallas kernels: 136 us -> 124 us
  local copies, waits for them, and re-layouts: 3.64 us -> 0 us
  between operations: 2.39 us -> 0.64 us
    pallas_call x1 -> x2, Pallas kernels: 136 us -> 124 us  [the longest x1 123 us: body(): pl.pallas_call(program_body, out_shape=jax.ShapeDtypeStruct((8, ROWS), F3...]
    unnamed x2 -> x0, local copies, waits for them, and re-layouts: 2.32 us -> none
where the time goes in v2:
time: 125 us
  Pallas kernels  124 us (99%)
    pallas_call x1, Pallas kernels, body(): pl.pallas_call(program_body, out_shape=jax.ShapeDtypeStruct((8, ROWS), F3...  123 us

profile of v2, /device:TPU:1, one launch (start us, length us, event | category | flops | bytes accessed | tf_op | source)
XLA Modules:
  0.0 124.9 jit_solution(14097871742464696832)
XLA Ops:
  0.6 123.1 %shard_map.157.answer_ref = f32[8,128]{1,0:T(8,128)} custom-call(bf16[4,8192]{1,0:T(4,128)(2,1)} %bitcast.8, bf16[128,1024]{1,0:T(8,128)(2,1)} %bitcast.6, bf16[128,1024]{1,0:T(8,128)(2,1)} %bitcast.7, s32[32,128]{1,0:T(8,128)} %bitcast.10, s32[1,128]{1,0:T(1,128)} %par_hbm.1, s32[1,128]{1,0:T(1,128)} %pos_hbm.1, bf16[256,5120]{1,0:T(8,128)(2,1)} %ow_hbm.1, ...), custom_call_target="tpu_custom_call" | custom-call | tf_op jit(solution)/shard_map/pallas_call | solution.py:923
  123.7 1.2 shard_map.158

commit v3 on v2

--- a/solution.py
+++ b/solution.py
@@ -223,7 +223,7 @@
             mixed = mm(probs.T.astype(BF16), v_ref[:, lanes]).reshape(SLOTS, 4, 8, HEAD)
             for pair in range(4):
                 osend[at, pair] = mixed[0:WINDOW, pair].reshape(8 * WINDOW, HEAD)
-            for delta in (1, 3, 2):
+            for delta in (2, 1, 3):
                 send(
                     osend.at[at, lax.rem(x + delta, X)],
                     oxr.at[at, delta - 1],
@@ -328,7 +328,7 @@
     sorted_rows = mm(hot(in_row == from_row), stacked).astype(BF16)
     left = jnp.concatenate([sorted_rows[0:ROWS], sorted_rows[ROWS : 2 * ROWS]], axis=1)
     mixs[...] = left
-    for delta in (1, 3, 2):
+    for delta in (2, 1, 3):
         send(mixs, mixr.at[delta - 1], m_ss.at[delta - 1], m_rs.at[delta - 1], at_x(delta))
     own_weight.wait()
     product = mm(left, wown[...])
@@ -343,7 +343,7 @@
         product = product + mm(mixr[delta - 1], wx[delta - 1])
     zown[...] = product
 
-    for delta in (1, 7, 2, 6, 3, 5, 4):
+    for delta in (4, 3, 5, 2, 6, 1, 7):
         target = lax.rem(z + delta, Z)
         zsend[delta] = encode(zown[pl.ds(pl.multiple_of(16 * target, 16), 16), :])
         send(zsend.at[delta], zrecv.at[delta], z_ss.at[delta], z_rs.at[delta], at_z(delta))
@@ -351,12 +351,12 @@
     for delta in range(1, X):
         landed(rrecv.at[delta - 1], r_ss.at[delta], r_rs.at[delta], at_x(delta))
         hidden = hidden + rrecv[delta - 1].astype(F32)
-    for delta in (1, 7, 2, 6, 3, 5, 4):
+    for delta in (7, 1, 6, 2, 5, 3, 4):
         landed(zrecv.at[delta], z_ss.at[delta], z_rs.at[delta], at_z(delta))
         hidden = hidden + decode(zrecv[delta])
     squares = jnp.sum(hidden * hidden, axis=1, keepdims=True)
     sqs[...] = jnp.broadcast_to(squares, sqs.shape)
-    for delta in (1, 3, 2):
+    for delta in (2, 1, 3):
         send(sqs, sqr.at[delta - 1], s_ss.at[delta - 1], s_rs.at[delta - 1], at_x(delta))
     gain = gain_ref[dx_cols(x)].astype(F32).reshape(1, DX)
     for delta in (1, 3, 2):
@@ -440,6 +440,7 @@
 
 
 SIZE = {"x": X, "y": Y, "z": Z}
+DIRECT = "xy"
 
 
 def plan_gather():
@@ -455,6 +456,16 @@
                 amount *= SIZE[name]
             if chunked:
                 amount //= SIZE[order[1]]
+            if stage == 0 and axis in DIRECT:
+                for step in range(1, count):
+                    by_key[part, stage, step, None, 1] = len(messages)
+                    messages.append(
+                        dict(
+                            part=part, stage=stage, axis=axis, step=step, chunk=None, way=1, half=None,
+                            size=amount, hops=min(step, count - step), link=1 if 2 * step <= count else -1, direct=True,
+                        )
+                    )
+                continue
             for step in range(1, count // 2 + 1):
                 for rank, chunk in enumerate(inner):
                     for way in (1, -1):
@@ -473,7 +484,7 @@
                         messages.append(
                             dict(
                                 part=part, stage=stage, axis=axis, step=step, chunk=chunk, way=way, half=half,
-                                size=amount if half is None else amount // 2,
+                                size=amount if half is None else amount // 2, hops=1, link=way, direct=False,
                             )
                         )
 
@@ -493,7 +504,7 @@
 
     for message in messages:
         part, stage = message["part"], message["stage"]
-        if message["step"] > 1:
+        if message["step"] > 1 and not message["direct"]:
             if message["chunk"] is None:
                 needs = bringing(part, stage, -message["way"] * (message["step"] - 1))
             else:
@@ -532,13 +543,13 @@
             message = messages[index]
             if all(need in arrive for need in message["needs"]):
                 at = max([arrive[need] for need in message["needs"]], default=0.0)
-                link = (message["axis"], message["way"])
+                link = (message["axis"], message["link"])
                 begin = max(at, free.get(link, 0.0))
                 if best is None or (begin, at, index) < best[0]:
                     best = ((begin, at, index), index, link, at)
         (begin, at, unused), index, link, at = best
         left.remove(index)
-        finish = begin + messages[index]["size"] / 46e3
+        finish = begin + messages[index]["hops"] * messages[index]["size"] / 46e3
         free[link] = finish
         ready[index] = at
         arrive[index] = finish + 0.9
@@ -686,7 +697,7 @@
             dst_ref=ref,
             send_sem=g_ss.at[index],
             recv_sem=g_rs.at[index],
-            device_id=peer(message["axis"], message["way"]),
+            device_id=peer(message["axis"], message["step"] if message["direct"] else message["way"]),
         )
 
     def head_task(task):
@@ -789,7 +800,8 @@
     for unused, kind, index in events:
         if kind == 0:
             await_all(messages[index]["needs"])
-            copy = ring(index, -messages[index]["way"] * (messages[index]["step"] - 1))
+            back = 0 if messages[index]["direct"] else messages[index]["step"] - 1
+            copy = ring(index, -messages[index]["way"] * back)
             copy.start()
             pending.append(copy)
         else:

time: 125 us -> 124 us (level)
    pallas_call x1, Pallas kernels: 123 us -> 122 us  [body(): pl.pallas_call(program_body, out_shape=jax.ShapeDtypeStruct((8, ROWS), F3...]
where the time goes in v3:
time: 124 us
  Pallas kernels  123 us (99%)
    pallas_call x1, Pallas kernels, body(): pl.pallas_call(program_body, out_shape=jax.ShapeDtypeStruct((8, ROWS), F3...  122 us

profile of v3, /device:TPU:1, one launch (start us, length us, event | category | flops | bytes accessed | tf_op | source)
XLA Modules:
  0.0 123.5 jit_solution(809395930689383011)
XLA Ops:
  0.6 121.7 %shard_map.157.answer_ref = f32[8,128]{1,0:T(8,128)} custom-call(bf16[4,8192]{1,0:T(4,128)(2,1)} %bitcast.8, bf16[128,1024]{1,0:T(8,128)(2,1)} %bitcast.6, bf16[128,1024]{1,0:T(8,128)(2,1)} %bitcast.7, s32[32,128]{1,0:T(8,128)} %bitcast.10, s32[1,128]{1,0:T(1,128)} %par_hbm.1, s32[1,128]{1,0:T(1,128)} %pos_hbm.1, bf16[256,5120]{1,0:T(8,128)(2,1)} %ow_hbm.1, ...), custom_call_target="tpu_custom_call" | custom-call | tf_op jit(solution)/shard_map/pallas_call | solution.py:935
  122.3 1.2 shard_map.158
